TPU v7x, 32 devices: a whole 2x2x4 slice. The times are simulated.
32 devices in a mesh: pix: 16 (over z, x, core), ch: 2 (over y).
Axes of the slice: x: 2, y: 2, z: 4, core: 2. Of those that a mesh axis runs over, the one named last changes fastest.
Arguments:
- features: float32 [1536, 64, 256], P('pix', None, 'ch'), may hold values from -250 to 250, as said below
- sea_mask: int32 [1536, 64], P('pix'), may hold values from 0 to 1, as said below
- edge_flip: int32 [4, 2], replicated, may hold values from 0 to 1
- w_first: float32 [3, 3, 256, 256], P(None, None, None, 'ch'), may hold values from -0.125 to 0.125
- b_first: float32 [256], P('ch'), may hold values from -1.5 to 1.5
- w_second: float32 [3, 3, 256, 256], P(None, None, None, 'ch'), may hold values from -0.125 to 0.125
- b_second: float32 [256], P('ch'), may hold values from -1.5 to 1.5
- w_skip: float32 [256, 256], P(None, 'ch'), may hold values from -0.375 to 0.375
- b_skip: float32 [256], P('ch'), may hold values from -1.5 to 1.5
- run_mean: float32 [256], P('ch'), may hold values from -4 to 4
- run_var: float32 [256], P('ch'), may hold values from 0.5 to 20
- cotangent: float32 [1536, 64, 256], P('pix', None, 'ch'), may hold values from -6 to 6
Outputs:
- output: float32 [1536, 64, 256], P('pix', None, 'ch')
- grad_features: float32 [1536, 64, 256], P('pix', None, 'ch')
- grad_w_first: float32 [3, 3, 256, 256], P(None, None, None, 'ch')
- grad_b_first: float32 [256], P('ch')
- grad_w_second: float32 [3, 3, 256, 256], P(None, None, None, 'ch')
- grad_b_second: float32 [256], P('ch')
- grad_w_skip: float32 [256, 256], P(None, 'ch')
- grad_b_skip: float32 [256], P('ch')
- new_mean: float32 [256], P('ch')
- new_var: float32 [256], P('ch')
Inputs may be any that keep to these rules, and one draw needn't show every extreme that they name: `features`: channels of one field, scaled. `sea_mask`: 1 marks a valid sea pixel; the share of sea pixels is drawn for each face. `edge_flip`: entry [r, 0] reverses ribbon r's top rim, entry [r, 1] its bottom rim.
All inputs are finite; a program needn't handle non-finite values.
Results may differ from a plain program's by a relative error of at most 0.0003.
Values sent between devices are 32-bit elements; how exact they have to be, the bound alone decides.
No kernel may reach another device: no remote copies, remote signals or barrier semaphores. Data moves between devices by JAX's collectives and lax.ppermute only.
A program may use at most 256 MiB of HBM per device.

v0:
```python
import jax
import jax.numpy as jnp
from jax import lax
from jax.sharding import PartitionSpec as P

STRIPS = 2


EPSILON = 1e-05
MOMENTUM = 0.1
HIGHEST = lax.Precision.HIGHEST
INV_ROOT_TWO_PI = 0.3989422804014327
SQRT_HALF = 0.7071067811865476


def shifted(value, axis, steps):
    count = lax.axis_size(axis)
    pairs = [(source, (source + steps) % count) for source in range(count)]
    return lax.ppermute(value, axis, pairs)


def from_device(piece, offset):
    return shifted(piece, "pix", offset)


def back_to_device(piece, offset):
    return shifted(piece, "pix", offset)


def rows_from(piece, offset):
    return from_device(piece, offset)


def rows_back(piece, offset):
    return back_to_device(piece, offset)


def gelu_slope(values):
    return (
        0.5 * (1.0 + lax.erf(values * SQRT_HALF))
        + values * jnp.exp(-0.5 * values * values) * INV_ROOT_TWO_PI
    )


def pad_faces(values, placing):
    ribbon, at_top, at_bottom, flip_top, flip_bottom = placing
    height, breadth = (values.shape[0], values.shape[1])
    ahead = jnp.concatenate([values[:, 0, :], values[0], values[-1]], axis=0)
    behind = values[:, -1, :]
    from_next = jnp.where(ribbon == 3, from_device(ahead, 3 * STRIPS), from_device(ahead, -STRIPS))
    from_prev = jnp.where(
        ribbon == 0, from_device(behind, -3 * STRIPS), from_device(behind, STRIPS)
    )
    middle = jnp.concatenate([from_prev[:, None, :], values, from_next[:height, None, :]], axis=1)
    pole_top = from_next[height : height + breadth]
    pole_bottom = from_next[height + breadth :]
    pole_top = jnp.where(flip_top, pole_top[::-1], pole_top)
    pole_bottom = jnp.where(flip_bottom, pole_bottom[::-1], pole_bottom)
    top_pole = jnp.concatenate(
        [0.5 * (pole_top[:1] + middle[0, :1]), pole_top, 0.5 * (pole_top[-1:] + middle[0, -1:])],
        axis=0,
    )
    bottom_pole = jnp.concatenate(
        [
            0.5 * (pole_bottom[:1] + middle[-1, :1]),
            pole_bottom,
            0.5 * (pole_bottom[-1:] + middle[-1, -1:]),
        ],
        axis=0,
    )
    from_above = rows_from(middle[-1], 1)
    from_below = rows_from(middle[0], -1)
    upper_rim = jnp.where(at_top, top_pole, from_above)
    lower_rim = jnp.where(at_bottom, bottom_pole, from_below)
    return jnp.concatenate([upper_rim[None], middle, lower_rim[None]], axis=0)


def unpad_faces(grad, placing):
    ribbon, at_top, at_bottom, flip_top, flip_bottom = placing
    height, breadth = (grad.shape[0] - 2, grad.shape[1] - 2)
    grad_upper, grad_middle, grad_lower = (grad[0], grad[1:-1], grad[-1])
    grad_top_pole = jnp.where(at_top, grad_upper, 0.0)
    grad_bottom_pole = jnp.where(at_bottom, grad_lower, 0.0)
    grad_middle = grad_middle.at[-1].add(rows_back(jnp.where(at_top, 0.0, grad_upper), -1))
    grad_middle = grad_middle.at[0].add(rows_back(jnp.where(at_bottom, 0.0, grad_lower), 1))
    grad_middle = (
        grad_middle.at[0, 0].add(0.5 * grad_top_pole[0]).at[0, -1].add(0.5 * grad_top_pole[-1])
    )
    grad_middle = (
        grad_middle.at[-1, 0]
        .add(0.5 * grad_bottom_pole[0])
        .at[-1, -1]
        .add(0.5 * grad_bottom_pole[-1])
    )
    grad_pole_top = (
        grad_top_pole[1:-1].at[0].add(0.5 * grad_top_pole[0]).at[-1].add(0.5 * grad_top_pole[-1])
    )
    grad_pole_bottom = (
        grad_bottom_pole[1:-1]
        .at[0]
        .add(0.5 * grad_bottom_pole[0])
        .at[-1]
        .add(0.5 * grad_bottom_pole[-1])
    )
    grad_pole_top = jnp.where(flip_top, grad_pole_top[::-1], grad_pole_top)
    grad_pole_bottom = jnp.where(flip_bottom, grad_pole_bottom[::-1], grad_pole_bottom)
    grad_next = jnp.concatenate([grad_middle[:, -1], grad_pole_top, grad_pole_bottom], axis=0)
    grad_prev = grad_middle[:, 0]
    grad_values = grad_middle[:, 1:-1]
    grad_ahead = back_to_device(
        jnp.where(ribbon == 3, grad_next, 0.0), -3 * STRIPS
    ) + back_to_device(jnp.where(ribbon == 3, 0.0, grad_next), STRIPS)
    grad_behind = back_to_device(
        jnp.where(ribbon == 0, grad_prev, 0.0), 3 * STRIPS
    ) + back_to_device(jnp.where(ribbon == 0, 0.0, grad_prev), -STRIPS)
    grad_values = grad_values.at[:, 0].add(grad_ahead[:height])
    grad_values = grad_values.at[0].add(grad_ahead[height : height + breadth])
    grad_values = grad_values.at[-1].add(grad_ahead[height + breadth :])
    return grad_values.at[:, -1].add(grad_behind)


def padded_full(values, placing):
    return pad_faces(lax.all_gather(values, "ch", axis=2, tiled=True), placing)


def owned_grad(grad, placing):
    return lax.psum_scatter(unpad_faces(grad, placing), "ch", scatter_dimension=2, tiled=True)


def masked_stats(sea_weight, features):
    sea_count, totals = lax.psum(
        (jnp.sum(sea_weight), jnp.sum(sea_weight * features, axis=(0, 1))), "pix"
    )
    batch_mean = totals / sea_count
    centred = features - batch_mean
    batch_var = lax.psum(jnp.sum(sea_weight * centred * centred, axis=(0, 1)), "pix") / sea_count
    return (sea_count, batch_mean, batch_var, centred)


def conv_three(padded, kernel):
    height = padded.shape[0] - 2
    breadth = padded.shape[1] - 2
    summed = jnp.zeros((height, breadth, kernel.shape[3]), jnp.float32)
    for row_tap in range(3):
        for col_tap in range(3):
            window = padded[row_tap : row_tap + height, col_tap : col_tap + breadth, :]
            summed = summed + jnp.einsum(
                "hwi,io->hwo", window, kernel[row_tap, col_tap], precision=HIGHEST
            )
    return summed


def tap_grads(padded, grad):
    height, breadth = (grad.shape[0], grad.shape[1])
    return jnp.stack(
        [
            jnp.stack(
                [
                    jnp.einsum(
                        "hwi,hwo->io",
                        padded[row_tap : row_tap + height, col_tap : col_tap + breadth, :],
                        grad,
                        precision=HIGHEST,
                    )
                    for col_tap in range(3)
                ]
            )
            for row_tap in range(3)
        ]
    )


def conv_back(grad, kernel):
    height, breadth = (grad.shape[0], grad.shape[1])
    summed = jnp.zeros((height + 2, breadth + 2, kernel.shape[2]), jnp.float32)
    for row_tap in range(3):
        for col_tap in range(3):
            contrib = jnp.einsum("hwo,io->hwi", grad, kernel[row_tap, col_tap], precision=HIGHEST)
            summed = summed.at[row_tap : row_tap + height, col_tap : col_tap + breadth].add(contrib)
    return summed


def local(
    features,
    sea_mask,
    edge_flip,
    w_first,
    b_first,
    w_second,
    b_second,
    w_skip,
    b_skip,
    run_mean,
    run_var,
    cotangent,
):
    device_index = lax.axis_index("pix")
    ribbon = device_index // STRIPS % 4
    strip_index = device_index % STRIPS
    chosen_flags = jnp.sum(jnp.where((jnp.arange(4) == ribbon)[:, None], edge_flip, 0), axis=0)
    at_top = strip_index == 0
    at_bottom = strip_index == STRIPS - 1
    placing = (ribbon, at_top, at_bottom, chosen_flags[0] == 1, chosen_flags[1] == 1)
    sea_weight = sea_mask.astype(jnp.float32)[:, :, None]
    sea_count, batch_mean, batch_var, centred = masked_stats(sea_weight, features)
    inverse = lax.rsqrt(batch_var + EPSILON)
    normed = centred * inverse
    scaled_in = sea_weight * normed
    input_padded = padded_full(scaled_in, placing)
    input_full = input_padded[1:-1, 1:-1]
    pre_first = conv_three(input_padded, w_first) + b_first
    hidden = jax.nn.gelu(pre_first, approximate=False)
    hidden_padded = padded_full(hidden, placing)
    pre_second = conv_three(hidden_padded, w_second) + b_second
    skip_term = jnp.einsum("hwi,io->hwo", input_full, w_skip, precision=HIGHEST)
    output = jax.nn.gelu(pre_second, approximate=False) + skip_term + b_skip
    grad_second = cotangent * gelu_slope(pre_second)
    gw_second = tap_grads(hidden_padded, grad_second)
    gb_second = jnp.sum(grad_second, axis=(0, 1))
    grad_hidden = owned_grad(conv_back(grad_second, w_second), placing)
    grad_first = grad_hidden * gelu_slope(pre_first)
    gw_first = tap_grads(input_padded, grad_first)
    gb_first = jnp.sum(grad_first, axis=(0, 1))
    gw_skip = jnp.einsum("hwi,hwo->io", input_full, cotangent, precision=HIGHEST)
    gb_skip = jnp.sum(cotangent, axis=(0, 1))
    back_padded = conv_back(grad_first, w_first)
    back_padded = back_padded.at[1:-1, 1:-1].add(
        jnp.einsum("hwo,io->hwi", cotangent, w_skip, precision=HIGHEST)
    )
    grad_in = owned_grad(back_padded, placing)
    masked_grad = sea_weight * grad_in
    first_sum = jnp.sum(masked_grad, axis=(0, 1))
    second_sum = jnp.sum(masked_grad * normed, axis=(0, 1))
    gw_first, gb_first, gw_second, gb_second, gw_skip, gb_skip, first_sum, second_sum = lax.psum(
        (gw_first, gb_first, gw_second, gb_second, gw_skip, gb_skip, first_sum, second_sum), "pix"
    )
    grad_features = (
        sea_weight * inverse * (grad_in - first_sum / sea_count - normed * second_sum / sea_count)
    )
    new_mean = (1.0 - MOMENTUM) * run_mean + MOMENTUM * batch_mean
    new_var = (1.0 - MOMENTUM) * run_var + MOMENTUM * batch_var * sea_count / (sea_count - 1.0)
    return (
        output,
        grad_features,
        gw_first,
        gb_first,
        gw_second,
        gb_second,
        gw_skip,
        gb_skip,
        new_mean,
        new_var,
    )


def solution(mesh):
    placed = (
        P("pix", None, "ch"),
        P("pix", None),
        P(),
        P(None, None, None, "ch"),
        P("ch"),
        P(None, None, None, "ch"),
        P("ch"),
        P(None, "ch"),
        P("ch"),
        P("ch"),
        P("ch"),
        P("pix", None, "ch"),
    )
    return jax.shard_map(
        local,
        mesh=mesh,
        in_specs=placed,
        out_specs=(
            P("pix", None, "ch"),
            P("pix", None, "ch"),
            P(None, None, None, "ch"),
            P("ch"),
            P(None, None, None, "ch"),
            P("ch"),
            P(None, "ch"),
            P("ch"),
            P("ch"),
            P("ch"),
        ),
        check_vma=False,
    )
```

profile of v0, /device:TPU:0, one launch (start us, length us, event | category | flops | bytes accessed | tf_op | source)
XLA Modules:
  0.0 1718.3 jit_solution(17365991414512558479)
XLA Ops:
  13.6 35.6 %all-reduce.3 = (f32[128]{0:T(128)S(1)}, f32[]{:T(128)}) all-reduce(f32[128]{0:T(128)S(1)} %multiply_reduce_fusion.1, f32[]{:T(128)} %convert_reduce_fusion), channel_id=1, replica_groups=mesh['pix'=16,'ch'=2] {'pix'}, use_global_device_ids=true, to_apply=%region_2.3 | all-reduce | flops 129 | bytes 1032 | tf_op jit(solution)/shard_map/psum | solution.py:131
  53.8 29.5 %psum.79 = f32[128]{0:T(128)S(1)} all-reduce(f32[128]{0:T(128)S(1)} %fusion.36), channel_id=1, replica_groups=mesh['pix'=16,'ch'=2] {'pix'}, use_global_device_ids=true, to_apply=%region_6.7 | all-reduce | flops 128 | bytes 1024 | tf_op jit(solution)/shard_map/psum | solution.py:136
  93.6 75.1 %all-gather.3.cloned.1.call-done = f32[96,64,256]{2,0,1:T(8,128)} async-done(((f32[96,64,128]{2,0,1:T(8,128)}), f32[96,64,256]{2,0,1:T(8,128)}) %all-gather.3.cloned.1.call-update) | async-done | bytes 6291472 | tf_op jit(solution)/shard_map/all_gather | solution.py:123
  219.4 28.1 %fusion.250 = (f32[96,64,256]{2,1,0:T(8,128)}, f32[96,64,256]{2,1,0:T(8,128)}, f32[96,64,256]{2,1,0:T(8,128)}, f32[96,64,256]{2,1,0:T(8,128)}, f32[96,64,256]{2,1,0:T(8,128)}, /*index=5*/f32[96,64,256]{2,1,0:T(8,128)}) fusion(f32[97,66,256]{2,1,0:T(8,128)} %get-tuple-element.638, f32[97,66,256]{2,1,0:T(8,128)} %get-tuple-element.637), kind=kLoop, calls=%fused_computation.435 | loop fusion | bytes 75497472 | tf_op jit(solution)/shard_map/slice | solution.py:146
  299.5 18.3 %fusion.38 = (f32[96,64,128]{2,0,1:T(8,128)}, f32[96,64,128]{2,0,1:T(8,128)}) fusion(f32[128]{0:T(128)S(1)} %copy-done.53, f32[3,3,256,128]{3,2,1,0:T(8,128)S(1)} %copy-done.19, f32[96,64,256]{2,1,0:T(8,128)S(1)} %bitcast.372, f32[96,64,128]{2,0,1:T(8,128)} %fusion.18, f32[96,64,128]{2,0,1:T(8,128)} %fusion.20, f32[96,64,128]{2,0,1:T(8,128)} %fusion.32, ...), kind=kOutput, calls=%fused_computation.68 | convolution fusion | flops 2473328640 | bytes 37880320 | tf_op jit(solution)/shard_map/hwi,io->hwo/dot_general | solution.py:147
  320.5 78.1 %all-gather.5.cloned.1.call-done = f32[96,64,256]{2,0,1:T(8,128)} async-done(((f32[96,64,128]{2,0,1:T(8,128)}), f32[96,64,256]{2,0,1:T(8,128)}) %all-gather.5.cloned.1.call-update) | async-done | bytes 6291472 | tf_op jit(solution)/shard_map/all_gather | solution.py:123
  512.9 17.4 %fusion.244 = (f32[128]{0:T(128)}, f32[96,64,128]{2,0,1:T(8,128)S(1)}, f32[96,64,128]{2,0,1:T(8,128)}) fusion(f32[96,64,128]{2,1,0:T(8,128)S(1)} %copy-done.12, f32[128]{0:T(128)S(1)} %copy-done.48, f32[3,3,256,128]{3,2,1,0:T(8,128)} %param.111, f32[96,64,256]{2,1,0:T(8,128)S(1)} %copy-done.17, f32[96,64,128]{2,0,1:T(8,128)} %fusion.6, ...), kind=kOutput, calls=%fused_computation.431 | convolution fusion | flops 2430861312 | bytes 41026560 | tf_op jit(solution)/shard_map/hwi,io->hwo/dot_general | solution.py:147
  550.9 31.5 %scatter-add.159 = f32[98,66,256]{2,1,0:T(8,128)} dynamic-update-slice(f32[98,66,256]{2,1,0:T(8,128)} %scatter-add.156, f32[96,64,256]{2,1,0:T(8,128)} %dynamic-slice_add_fusion.1, s32[]{:T(128)} %bitcast.58, s32[]{:T(128)} %bitcast.59, s32[]{:T(128)} %constant.1179.clone.1) | dynamic-update-slice | bytes 12582916 | tf_op jit(solution)/shard_map/scatter-add | solution.py:179
  595.2 31.5 %scatter-add.160 = f32[98,66,256]{2,1,0:T(8,128)} dynamic-update-slice(f32[98,66,256]{2,1,0:T(8,128)} %scatter-add.159, f32[96,64,256]{2,1,0:T(8,128)} %add_select_fusion.1, s32[]{:T(128)} %bitcast.61, s32[]{:T(128)} %bitcast.62, s32[]{:T(128)} %constant.1179.clone.1) | dynamic-update-slice | bytes 12582916 | tf_op jit(solution)/shard_map/scatter-add | solution.py:179
  646.5 30.3 %scatter-add.164 = f32[98,66,256]{2,1,0:T(8,128)} dynamic-update-slice(f32[98,66,256]{2,1,0:T(8,128)} %fusion.3, f32[96,64,256]{2,1,0:T(8,128)} %slice_add_fusion.11, s32[]{:T(128)} %constant.1180.clone.1, s32[]{:T(128)} %constant.1180.clone.1, s32[]{:T(128)} %constant.1179.clone.1) | dynamic-update-slice | bytes 12582916 | tf_op jit(solution)/shard_map/scatter-add | solution.py:179
  687.4 30.3 %scatter-add.165 = f32[98,66,256]{2,1,0:T(8,128)} dynamic-update-slice(f32[98,66,256]{2,1,0:T(8,128)} %scatter-add.164, f32[96,64,256]{2,1,0:T(8,128)} %slice_add_fusion.10, s32[]{:T(128)} %constant.1180.clone.1, s32[]{:T(128)} %constant.1181.clone.1, s32[]{:T(128)} %constant.1179.clone.1) | dynamic-update-slice | bytes 12582916 | tf_op jit(solution)/shard_map/scatter-add | solution.py:179
  737.5 30.3 %scatter-add.169 = f32[98,66,256]{2,1,0:T(8,128)} dynamic-update-slice(f32[98,66,256]{2,1,0:T(8,128)} %fusion.2, f32[96,64,256]{2,1,0:T(8,128)} %slice_add_fusion.8, s32[]{:T(128)} %constant.1181.clone.1, s32[]{:T(128)} %constant.1180.clone.1, s32[]{:T(128)} %constant.1179.clone.1) | dynamic-update-slice | bytes 12582916 | tf_op jit(solution)/shard_map/scatter-add | solution.py:179
  778.5 30.3 %scatter-add.170 = f32[98,66,256]{2,1,0:T(8,128)} dynamic-update-slice(f32[98,66,256]{2,1,0:T(8,128)} %scatter-add.169, f32[96,64,256]{2,1,0:T(8,128)} %slice_add_fusion.7, s32[]{:T(128)} %constant.1181.clone.1, s32[]{:T(128)} %constant.1181.clone.1, s32[]{:T(128)} %constant.1179.clone.1) | dynamic-update-slice | bytes 12582916 | tf_op jit(solution)/shard_map/scatter-add | solution.py:179
  884.1 76.4 %reduce-scatter.3.cloned.1.call-done = f32[96,64,128]{2,0,1:T(8,128)} async-done(((f32[96,64,256]{2,0,1:T(8,128)}), f32[96,64,128]{2,0,1:T(8,128)}) %reduce-scatter.3.cloned.1.call-update) | async-done | bytes 3145744 | tf_op jit(solution)/shard_map/reduce_scatter | solution.py:127
  985.6 31.5 %scatter-add.196 = f32[98,66,256]{2,1,0:T(8,128)} dynamic-update-slice(f32[98,66,256]{2,1,0:T(8,128)} %scatter-add.195, f32[96,64,256]{2,1,0:T(8,128)} %dynamic-slice_add_fusion, s32[]{:T(128)} %bitcast.58, s32[]{:T(128)} %bitcast.59, s32[]{:T(128)} %constant.1179.clone.1) | dynamic-update-slice | bytes 12582916 | tf_op jit(solution)/shard_map/scatter-add | solution.py:179
  1028.9 31.5 %scatter-add.199 = f32[98,66,256]{2,1,0:T(8,128)} dynamic-update-slice(f32[98,66,256]{2,1,0:T(8,128)} %scatter-add.196, f32[96,64,256]{2,1,0:T(8,128)} %add_select_fusion, s32[]{:T(128)} %bitcast.61, s32[]{:T(128)} %bitcast.62, s32[]{:T(128)} %constant.1179.clone.1) | dynamic-update-slice | bytes 12582916 | tf_op jit(solution)/shard_map/scatter-add | solution.py:179
  1081.5 30.3 %scatter-add.201 = f32[98,66,256]{2,1,0:T(8,128)} dynamic-update-slice(f32[98,66,256]{2,1,0:T(8,128)} %fusion.1, f32[96,64,256]{2,1,0:T(8,128)} %slice_add_fusion.5, s32[]{:T(128)} %constant.1180.clone.1, s32[]{:T(128)} %constant.1180.clone.1, s32[]{:T(128)} %constant.1179.clone.1) | dynamic-update-slice | bytes 12582916 | tf_op jit(solution)/shard_map/scatter-add | solution.py:179
  1121.7 30.3 %scatter-add.204 = f32[98,66,256]{2,1,0:T(8,128)} dynamic-update-slice(f32[98,66,256]{2,1,0:T(8,128)} %scatter-add.201, f32[96,64,256]{2,1,0:T(8,128)} %slice_add_fusion.4, s32[]{:T(128)} %constant.1180.clone.1, s32[]{:T(128)} %constant.1181.clone.1, s32[]{:T(128)} %constant.1179.clone.1) | dynamic-update-slice | bytes 12582916 | tf_op jit(solution)/shard_map/scatter-add | solution.py:179
  1173.1 30.3 %scatter-add.206 = f32[98,66,256]{2,1,0:T(8,128)} dynamic-update-slice(f32[98,66,256]{2,1,0:T(8,128)} %fusion, f32[96,64,256]{2,1,0:T(8,128)} %slice_add_fusion.2, s32[]{:T(128)} %constant.1181.clone.1, s32[]{:T(128)} %constant.1180.clone.1, s32[]{:T(128)} %constant.1179.clone.1) | dynamic-update-slice | bytes 12582916 | tf_op jit(solution)/shard_map/scatter-add | solution.py:179
  1213.5 30.3 %scatter-add.209 = f32[98,66,256]{2,1,0:T(8,128)} dynamic-update-slice(f32[98,66,256]{2,1,0:T(8,128)} %scatter-add.206, f32[96,64,256]{2,1,0:T(8,128)} %slice_add_fusion.1, s32[]{:T(128)} %constant.1181.clone.1, s32[]{:T(128)} %constant.1181.clone.1, s32[]{:T(128)} %constant.1179.clone.1) | dynamic-update-slice | bytes 12582916 | tf_op jit(solution)/shard_map/scatter-add | solution.py:179
  1253.2 30.3 %scatter-add.210 = f32[98,66,256]{2,1,0:T(8,128)} dynamic-update-slice(f32[98,66,256]{2,1,0:T(8,128)} %scatter-add.209, f32[96,64,256]{2,1,0:T(8,128)} %slice_add_fusion, s32[]{:T(128)} %constant.1180.clone.1, s32[]{:T(128)} %constant.1180.clone.1, s32[]{:T(128)} %constant.1179.clone.1) | dynamic-update-slice | bytes 12582916 | tf_op jit(solution)/shard_map/scatter-add | solution.py:227
  1363.3 16.8 fusion.79
  1612.4 33.8 %all-reduce.2 = (f32[128]{0:T(128)S(1)}, f32[128]{0:T(128)S(1)}, f32[128]{0:T(128)}, f32[128]{0:T(128)}, f32[128]{0:T(128)}) all-reduce(f32[128]{0:T(128)S(1)} %get-tuple-element.585, f32[128]{0:T(128)S(1)} %get-tuple-element.584, f32[128]{0:T(128)S(1)} %copy-done.46, ...), channel_id=1, replica_groups=mesh['pix'=16,'ch'=2] {'pix'}, use_global_device_ids=true, to_apply=%region_14.15 | all-reduce | flops 640 | bytes 5120 | tf_op jit(solution)/shard_map/psum | solution.py:234
  1654.9 52.5 %all-reduce.7.cloned.1.call-done = (f32[3,3,256,128]{3,2,1,0:T(8,128)}, f32[3,3,256,128]{3,2,1,0:T(8,128)}, f32[256,128]{1,0:T(8,128)}) async-done(((f32[3,3,256,128]{3,2,1,0:T(8,128)}, f32[3,3,256,128]{3,2,1,0:T(8,128)}, f32[256,128]{1,0:T(8,128)}), (f32[3,3,256,128]{3,2,1,0:T(8,128)}, f32[3,3,256,128]{3,2,1,0:T(8,128)}, f32[256,128]{1,0:T(8,128)})) %all-reduce.7.cloned.1.call-update) | async-done | bytes 2490384 | tf_op jit(solution)/shard_map/psum | solution.py:234
  (439 shorter events, 840.0 us)
Async XLA Ops:
  7.2 161.6 %all-gather.3.cloned.1.call-start = ((), (), s32[]{:S(2)}) async-start(), calls=%async_computation.2 | async-start | bytes 9437184 | tf_op jit(solution)/shard_map/all_gather | solution.py:123
  91.0 307.6 %all-gather.5.cloned.1.call-start = ((), (), s32[]{:S(2)}) async-start(), calls=%async_computation.3 | async-start | bytes 9437184 | tf_op jit(solution)/shard_map/all_gather | solution.py:123
  175.4 23.1 %collective-permute-start = (f32[224,256]{1,0:T(8,128)S(1)}, f32[224,256]{1,0:T(8,128)S(1)}, u32[]{:S(2)}, u32[]{:S(2)}) collective-permute-start(f32[224,256]{1,0:T(8,128)S(1)} %pad_maximum_fusion.24), channel_id=1, source_target_pairs={{0,12},{2,14},{4,16},{6,18},{8,20},{10,22},{12,24},{14,26},{16,28}... | collective-permute-start | bytes 688136 | tf_op jit(solution)/shard_map/ppermute | solution.py:19
  177.9 20.7 %collective-permute-start.1 = (f32[224,256]{1,0:T(8,128)S(1)}, f32[224,256]{1,0:T(8,128)S(1)}, u32[]{:S(2)}, u32[]{:S(2)}) collective-permute-start(f32[224,256]{1,0:T(8,128)S(1)} %pad_maximum_fusion.24), channel_id=1, source_target_pairs={{0,28},{2,30},{4,0},{6,2},{8,4},{10,6},{12,8},{14,10},{16,12},{18,... | collective-permute-start | bytes 688136 | tf_op jit(solution)/shard_map/ppermute | solution.py:19
  180.2 10.6 collective-permute-start.2
  181.8 9.9 collective-permute-start.3
  200.0 13.1 collective-permute-start.5
  317.8 642.7 %reduce-scatter.3.cloned.1.call-start = ((), (), s32[]{:S(2)}) async-start(), calls=%async_computation.4 | async-start | bytes 9437184 | tf_op jit(solution)/shard_map/reduce_scatter | solution.py:127
  399.5 24.4 %collective-permute-start.8 = (f32[96,256]{1,0:T(8,128)S(1)}, f32[96,256]{1,0:T(8,128)S(1)}, u32[]{:S(2)}, u32[]{:S(2)}) collective-permute-start(f32[96,256]{1,0:T(8,128)S(1)} %get-tuple-element.641), channel_id=1, source_target_pairs={{0,20},{2,22},{4,24},{6,26},{8,28},{10,30},{12,0},{14,2},{16,4},{1... | collective-permute-start | bytes 294920 | tf_op jit(solution)/shard_map/ppermute | solution.py:19
  402.9 21.0 %collective-permute-start.9 = (f32[96,256]{1,0:T(8,128)S(1)}, f32[96,256]{1,0:T(8,128)S(1)}, u32[]{:S(2)}, u32[]{:S(2)}) collective-permute-start(f32[96,256]{1,0:T(8,128)S(1)} %get-tuple-element.641), channel_id=1, source_target_pairs={{0,4},{2,6},{4,8},{6,10},{8,12},{10,14},{12,16},{14,18},{16,20},{1... | collective-permute-start | bytes 294920 | tf_op jit(solution)/shard_map/ppermute | solution.py:19
  405.8 25.1 %collective-permute-start.6 = (f32[224,256]{1,0:T(8,128)S(1)}, f32[224,256]{1,0:T(8,128)S(1)}, u32[]{:S(2)}, u32[]{:S(2)}) collective-permute-start(f32[224,256]{1,0:T(8,128)S(1)} %pad_maximum_fusion.25), channel_id=1, source_target_pairs={{0,12},{2,14},{4,16},{6,18},{8,20},{10,22},{12,24},{14,26},{16,28}... | collective-permute-start | bytes 688136 | tf_op jit(solution)/shard_map/ppermute | solution.py:19
  406.3 24.5 %collective-permute-start.7 = (f32[224,256]{1,0:T(8,128)S(1)}, f32[224,256]{1,0:T(8,128)S(1)}, u32[]{:S(2)}, u32[]{:S(2)}) collective-permute-start(f32[224,256]{1,0:T(8,128)S(1)} %pad_maximum_fusion.25), channel_id=1, source_target_pairs={{0,28},{2,30},{4,0},{6,2},{8,4},{10,6},{12,8},{14,10},{16,12},{18,... | collective-permute-start | bytes 688136 | tf_op jit(solution)/shard_map/ppermute | solution.py:19
  432.2 10.2 collective-permute-start.11
  809.8 10.8 collective-permute-start.12
  849.3 11.7 collective-permute-start.14
  849.4 14.3 collective-permute-start.15
  851.5 30.9 %collective-permute-start.16 = (f32[96,256]{1,0:T(8,128)}, f32[96,256]{1,0:T(8,128)}, u32[]{:S(2)}, u32[]{:S(2)}) collective-permute-start(f32[96,256]{1,0:T(8,128)} %get-tuple-element.666), channel_id=1, source_target_pairs={{0,12},{2,14},{4,16},{6,18},{8,20},{10,22},{12,24},{14,26},{16,28}... | collective-permute-start | bytes 294920 | tf_op jit(solution)/shard_map/ppermute | solution.py:19
  853.9 28.5 %collective-permute-start.17 = (f32[96,256]{1,0:T(8,128)}, f32[96,256]{1,0:T(8,128)}, u32[]{:S(2)}, u32[]{:S(2)}) collective-permute-start(f32[96,256]{1,0:T(8,128)} %get-tuple-element.665), channel_id=1, source_target_pairs={{0,28},{2,30},{4,0},{6,2},{8,4},{10,6},{12,8},{14,10},{16,12},{18,... | collective-permute-start | bytes 294920 | tf_op jit(solution)/shard_map/ppermute | solution.py:19
  884.0 722.0 %reduce-scatter.5.cloned.1.call-start = ((), (), s32[]{:S(2)}) async-start(), calls=%async_computation.5 | async-start | bytes 9437184 | tf_op jit(solution)/shard_map/reduce_scatter | solution.py:127
  1284.5 10.1 collective-permute-start.18
  1324.4 15.1 collective-permute-start.21
  1327.9 31.0 %collective-permute-start.23 = (f32[96,256]{1,0:T(8,128)}, f32[96,256]{1,0:T(8,128)}, u32[]{:S(2)}, u32[]{:S(2)}) collective-permute-start(f32[96,256]{1,0:T(8,128)} %fusion.196), channel_id=1, source_target_pairs={{0,28},{2,30},{4,0},{6,2},{8,4},{10,6},{12,8},{14,10},{16,12},{18,... | collective-permute-start | bytes 294920 | tf_op jit(solution)/shard_map/ppermute | solution.py:19
  1331.4 27.5 %collective-permute-start.22 = (f32[96,256]{1,0:T(8,128)}, f32[96,256]{1,0:T(8,128)}, u32[]{:S(2)}, u32[]{:S(2)}) collective-permute-start(f32[96,256]{1,0:T(8,128)} %bitcast.344), channel_id=1, source_target_pairs={{0,12},{2,14},{4,16},{6,18},{8,20},{10,22},{12,24},{14,26},{16,28}... | collective-permute-start | bytes 294920 | tf_op jit(solution)/shard_map/ppermute | solution.py:19
  1360.5 346.9 %all-reduce.7.cloned.1.call-start = ((), (), s32[]{:S(2)}) async-start(), calls=%async_computation.6 | async-start | bytes 4980736 | tf_op jit(solution)/shard_map/psum | solution.py:234
  (84 other events, 2630.7 us)
Sparse Core Ops, SparseCore 0:
  91.1 77.6 all-gather.2
  318.0 80.5 all-gather.4
  884.1 76.3 reduce-scatter.2
  1360.7 77.0 reduce-scatter.4
  1606.1 101.2 all-reduce.6
where the time goes:
time: 1740 us; the launch traced here: 1720 us
  matrix products  615 us (35%)
  local copies, waits for them, and re-layouts  554 us (32%)
  waiting for transfers between devices  299 us (17%)
  blocking collectives  98.8 us (6%)
  other arithmetic  92.6 us (5%)
  starting transfers between devices  41.3 us (2%)
  between operations  18.1 us (1%)
    scatter-add x14, local copies, waits for them, and re-layouts, conv_back(): summed.at[row_tap:row_tap + height, col_tap:col_tap + breadth].add(contrib)  375 us
    dot_general x18, matrix products, tap_grads(): jnp.einsum('hwi,hwo->io', padded[row_tap:row_tap + height, col_tap:col_ta...  207 us
    dot_general x18, matrix products, conv_three(): jnp.einsum('hwi,io->hwo', window, kernel[row_tap, col_tap], precision=HIG...  187 us
    dot_general x18, matrix products, conv_back(): jnp.einsum('hwo,io->hwi', grad, kernel[row_tap, col_tap], precision=HIGHEST)  182 us
    all_gather x2, waiting for transfers between devices, padded_full(): return pad_faces(lax.all_gather(values, 'ch', axis=2, tiled=True), placing)  153 us
    reduce_scatter x2, waiting for transfers between devices, owned_grad(): lax.psum_scatter(unpad_faces(grad, placing), 'ch', scatter_dimension=2, t...  76.5 us
    psum x1, waiting for transfers between devices, local(): lax.psum((gw_first, gb_first, gw_second, gb_second, gw_skip, gb_skip, fir...  52.5 us
    ppermute x24, starting transfers between devices, shifted(): return lax.ppermute(value, axis, pairs)  41.1 us
  transfers between devices with their start and end apart: 29, of which 10 were waited for; matrix products, arithmetic and copies ran while one was open for 22% of the time, Pallas kernels for 0%

commit v1 on v0

v1 whole, which is shorter than its diff:
```python
import functools

import jax
import jax.numpy as jnp
from jax import lax
from jax.experimental import pallas as pl
from jax.experimental.pallas import tpu as pltpu
from jax.sharding import PartitionSpec as P

EPSILON = 1e-05
MOMENTUM = 0.1
INV_ROOT_TWO_PI = 0.3989422804014327
SQRT_HALF = 0.7071067811865476
F32 = jnp.float32
BF16 = jnp.bfloat16
VMEM_LIMIT = 60 * 1024 * 1024


def split(value):
    high = value.astype(BF16)
    return high, (value - high.astype(F32)).astype(BF16)


def dot_split(a_high, a_low, b_high, b_low):
    total = jnp.dot(a_high, b_high, preferred_element_type=F32)
    total = total + jnp.dot(a_high, b_low, preferred_element_type=F32)
    return total + jnp.dot(a_low, b_high, preferred_element_type=F32)


def gelu_and_slope(u):
    cdf = 0.5 * (1.0 + lax.erf(u * SQRT_HALF))
    return u * cdf, cdf + u * jnp.exp(-0.5 * u * u) * INV_ROOT_TWO_PI


def put_shifts(high, low, block, value, left, right):
    breadth, depth = value.shape
    column = lax.broadcasted_iota(jnp.int32, (breadth, 1), 0)
    shifts = (
        jnp.where(column == 0, left, pltpu.roll(value, 1, 0)),
        value,
        jnp.where(column == breadth - 1, right, pltpu.roll(value, breadth - 1, 0)),
    )
    for tap, piece in enumerate(shifts):
        piece_high, piece_low = split(piece)
        high[pl.ds(block * breadth, breadth), tap * depth : (tap + 1) * depth] = piece_high
        low[pl.ds(block * breadth, breadth), tap * depth : (tap + 1) * depth] = piece_low


def conv_rows(high, low, w_high, w_low, first, rows, breadth):
    total = None
    for row_tap in range(3):
        window = pl.ds(pl.multiple_of((first + row_tap) * breadth, breadth), rows * breadth)
        part = dot_split(high[window, :], low[window, :], w_high[row_tap], w_low[row_tap])
        total = part if total is None else total + part
    return total


def put_padded(flags, x, left, right, pole, high, low, begin, count, top, bottom):
    breadth = x.shape[1]

    @pl.loop(0, count)
    def _(block):
        row = block + begin
        put_shifts(high, low, block, x[row], left[pl.ds(row, 1)], right[pl.ds(row, 1)])

    def put_pole(at, edge):
        corner_left = 0.5 * (pole[0:1] + left[edge : edge + 1])
        corner_right = 0.5 * (pole[breadth - 1 : breadth] + right[edge : edge + 1])
        put_shifts(high, low, at - begin, pole[...], corner_left, corner_right)

    @pl.when(flags[0] == 1)
    def _():
        put_pole(top, top + 1)

    @pl.when(flags[1] == 1)
    def _():
        put_pole(bottom, bottom - 1)


def first_kernel(flags, x, left, right, pole, w_high, w_low, bias, hidden, slope, high, low, *, tile):
    blocks, breadth = x.shape[0], x.shape[1]
    depth = hidden.shape[2]
    put_padded(flags, x, left, right, pole, high, low, 0, blocks, 3, blocks - 4)

    @pl.loop(0, (blocks - 2) // tile)
    def _(step):
        first = step * tile
        pre = conv_rows(high, low, w_high, w_low, first, tile, breadth) + bias[...]
        value, grad = gelu_and_slope(pre)
        hidden[pl.ds(first, tile)] = value.reshape(tile, breadth, depth)
        slope[pl.ds(first, tile)] = grad.reshape(tile, breadth, depth)


def second_kernel(
    flags, x, left, right, pole, w_high, w_low, bias, source, s_high, s_low, s_bias, out, slope, high, low, *, tile
):
    blocks, breadth = x.shape[0], x.shape[1]
    depth = out.shape[2]
    put_padded(flags, x, left, right, pole, high, low, 0, blocks, 2, blocks - 3)

    @pl.loop(0, (blocks - 2) // tile)
    def _(step):
        first = step * tile
        pre = conv_rows(high, low, w_high, w_low, first, tile, breadth) + bias[...]
        value, grad = gelu_and_slope(pre)
        skip_high, skip_low = split(source[pl.ds(first + 2, tile)].reshape(tile * breadth, -1))
        skip = dot_split(skip_high, skip_low, s_high[...], s_low[...]) + s_bias[...]
        out[pl.ds(first, tile)] = (value + skip).reshape(tile, breadth, depth)
        slope[pl.ds(first, tile)] = grad.reshape(tile, breadth, depth)


def back_conv(high, low, w_high, w_low, edge_first, edge_last, out, blocks, breadth, tile):
    depth = edge_first.shape[1]
    for tap in range(3):
        for edge, slot, base in ((edge_first, 2, blocks), (edge_last, 0, blocks + 3)):
            rows = pl.ds((base + tap) * breadth, breadth)
            edge_high, edge_low = split(edge[tap : tap + breadth])
            zero = jnp.zeros((breadth, 3 * depth), BF16)
            high[rows, :] = zero
            low[rows, :] = zero
            high[rows, slot * depth : (slot + 1) * depth] = edge_high
            low[rows, slot * depth : (slot + 1) * depth] = edge_low

    @pl.loop(0, (blocks + 4) // tile)
    def _(step):
        first = step * tile
        out[pl.ds(first, tile)] = conv_rows(high, low, w_high, w_low, first, tile, breadth).reshape(
            tile, breadth, depth
        )


def back_second_kernel(flags, cot, slope, w_high, w_low, out, grad, high, low, edge_first, edge_last, *, tile):
    blocks, breadth = cot.shape[0], cot.shape[1]
    edge_first[...] = jnp.zeros_like(edge_first)
    edge_last[...] = jnp.zeros_like(edge_last)

    @pl.loop(0, blocks)
    def _(block):
        outside = ((flags[0] == 1) & (block < 2)) | ((flags[1] == 1) & (block >= blocks - 2))
        value = cot[block] * slope[block] * jnp.where(outside, 0.0, 1.0)
        put_shifts(high, low, block, value, 0.0, 0.0)
        edge_first[pl.ds(block, 1)] = value[0:1]
        edge_last[pl.ds(block, 1)] = value[breadth - 1 : breadth]

        @pl.when((block >= 2) & (block < blocks - 2))
        def _():
            grad[block - 2] = value

    back_conv(high, low, w_high, w_low, edge_first, edge_last, out, blocks, breadth, tile)


def back_first_kernel(
    flags, upper, add_first, add_last, add_pole, slope, cot, w_high, w_low, s_high, s_low,
    out, grad, high, low, edge_first, edge_last, *, tile
):
    blocks, breadth, depth = cot.shape
    column = lax.broadcasted_iota(jnp.int32, (breadth, 1), 0)
    edge_first[...] = jnp.zeros_like(edge_first)
    edge_last[...] = jnp.zeros_like(edge_last)
    none = jnp.zeros((breadth, depth), F32)
    put_shifts(high, low, 0, none, 0.0, 0.0)
    put_shifts(high, low, blocks - 1, none, 0.0, 0.0)

    @pl.loop(1, blocks - 1)
    def _(block):
        row = block - 1
        outside = ((flags[0] == 1) & (block < 2)) | ((flags[1] == 1) & (block >= blocks - 2))
        edge = ((flags[0] == 1) & (block == 2)) | ((flags[1] == 1) & (block == blocks - 3))
        value = upper[row] + jnp.where(column == 0, add_first[pl.ds(row, 1)], 0.0)
        value = value + jnp.where(column == breadth - 1, add_last[pl.ds(row, 1)], 0.0)
        value = value + add_pole[...] * jnp.where(edge, 1.0, 0.0)
        value = value * slope[row + 2] * jnp.where(outside, 0.0, 1.0)
        put_shifts(high, low, block, value, 0.0, 0.0)
        edge_first[pl.ds(block, 1)] = value[0:1]
        edge_last[pl.ds(block, 1)] = value[breadth - 1 : breadth]

        @pl.when((block >= 2) & (block < blocks - 2))
        def _():
            grad[block - 2] = value

    back_conv(high, low, w_high, w_low, edge_first, edge_last, out, blocks, breadth, tile)

    @pl.loop(0, (blocks - 4) // tile)
    def _(step):
        first = step * tile
        cot_high, cot_low = split(cot[pl.ds(first + 2, tile)].reshape(tile * breadth, depth))
        skip = dot_split(cot_high, cot_low, s_high[...], s_low[...])
        out[pl.ds(first + 1, tile)] = out[pl.ds(first + 1, tile)] + skip.reshape(tile, breadth, depth)


def put_transposed(source, begin, rows, breadth, high, low, total, tile):
    depth = source.shape[2]
    total[...] = jnp.zeros_like(total)

    @pl.loop(0, rows // tile)
    def _(step):
        piece = source[pl.ds(begin + step * tile, tile)].reshape(tile * breadth, depth)
        total[...] += jnp.sum(piece, axis=0, keepdims=True)
        piece_high, piece_low = split(piece.T)
        window = pl.ds(pl.multiple_of(step * tile * breadth, tile * breadth), tile * breadth)
        high[:, window] = piece_high
        low[:, window] = piece_low


def put_weight_grad(out, at, grad, swap, depth):
    half = depth // 2
    out[at + (pl.ds(swap, half),)] = grad[:half]
    out[at + (pl.ds(half - swap, half),)] = grad[half:]


def weight_kernel(flags, x, left, right, pole, grad, *rest, begin, top, bottom, skip):
    if skip:
        cot, out, total, out_skip, total_skip, high, low, t_high, t_low = rest
    else:
        out, total, high, low, t_high, t_low = rest
    rows, breadth, depth = grad.shape
    put_padded(flags, x, left, right, pole, high, low, begin, rows + 2, top, bottom)
    put_transposed(grad, 0, rows, breadth, t_high, t_low, total, 4)
    swap = pl.multiple_of(flags[2] * (depth // 2), depth // 2)

    @pl.loop(0, 3)
    def _(row_tap):
        window = pl.ds(pl.multiple_of(row_tap * breadth, breadth), rows * breadth)
        for tap in range(3):
            lanes = slice(tap * depth, (tap + 1) * depth)
            part = dot_split(t_high[...], t_low[...], high[window, lanes], low[window, lanes])
            put_weight_grad(out, (row_tap, tap), part.T, swap, depth)

    if skip:
        put_transposed(cot, 2, rows, breadth, t_high, t_low, total_skip, 4)
        window, lanes = slice(breadth, breadth + rows * breadth), slice(depth, 2 * depth)
        part = dot_split(t_high[...], t_low[...], high[window, lanes], low[window, lanes])
        put_weight_grad(out_skip, (), part.T, swap, depth)


def call(kernel, shapes, scratch, flags, *operands):
    whole = pl.BlockSpec(memory_space=pltpu.VMEM)
    return pl.pallas_call(
        kernel,
        out_shape=[jax.ShapeDtypeStruct(shape, F32) for shape in shapes],
        in_specs=[pl.BlockSpec(memory_space=pltpu.SMEM)] + [whole] * len(operands),
        out_specs=[whole] * len(shapes),
        scratch_shapes=scratch,
        compiler_params=pltpu.CompilerParams(vmem_limit_bytes=VMEM_LIMIT),
    )(flags, *operands)


class Place:
    def __init__(self, mesh, rows, breadth):
        self.count = mesh.shape["pix"]
        self.strips = 3 * breadth // rows
        assert mesh.shape["ch"] == 2 and self.strips == 2
        self.pix = lax.axis_index("pix")
        self.side = lax.axis_index("ch")
        self.ribbon = self.pix // self.strips % 4
        self.strip = self.pix % self.strips
        self.half = self.side ^ self.strip
        self.at_top = (self.side == 0) & (self.strip == 0)
        self.at_bottom = (self.side == 0) & (self.strip == 1)
        self.at_pole = self.side == 0

    def ribbon_pairs(self, offset):
        pairs = []
        for index in range(self.count):
            sample, strip = index // (4 * self.strips), index % self.strips
            ribbon = (index // self.strips + offset) % 4
            pairs.append((index, (sample * 4 + ribbon) * self.strips + strip))
        return pairs

    def to_next(self, value):
        return lax.ppermute(value, "pix", self.ribbon_pairs(1))

    def to_prev(self, value):
        return lax.ppermute(value, "pix", self.ribbon_pairs(-1))

    def across(self, value):
        return lax.ppermute(value, "ch", [(0, 1), (1, 0)])

    def flip(self, value, bit):
        return lax.ppermute(value, "pix", [(i, i ^ bit) for i in range(self.count)])

    def bits(self):
        bit, out = 1, []
        while bit < self.count:
            out.append(bit)
            bit *= 2
        return out

    def ordered(self, mine, theirs, bit):
        upper = (self.pix & bit) != 0
        return jnp.where(upper, theirs, mine), jnp.where(upper, mine, theirs)

    def gathered(self, value):
        for bit in reversed(self.bits()):
            value = jnp.stack(self.ordered(value, self.flip(value, bit), bit))
        steps = len(self.bits())
        value = value.transpose(tuple(reversed(range(steps))) + tuple(range(steps, value.ndim)))
        return value.reshape((-1,) + value.shape[steps + 1 :])

    def reduced(self, value):
        for bit in self.bits():
            upper = (self.pix & bit) != 0
            size = value.shape[0] // 2
            low, high = value[:size], value[size:]
            value = jnp.where(upper, high, low) + self.flip(jnp.where(upper, low, high), bit)
        return value

    def spread(self, value):
        for bit in reversed(self.bits()):
            value = jnp.concatenate(self.ordered(value, self.flip(value, bit), bit), axis=0)
        return value

    def summed(self, value):
        for bit in self.bits():
            first, second = self.ordered(value, self.flip(value, bit), bit)
            value = first + second
        return value

    def halves(self, value, extra, size):
        length = size + extra
        mine = lax.dynamic_slice_in_dim(value, self.half * (size - extra), length, 0)
        theirs = lax.dynamic_slice_in_dim(value, (1 - self.half) * (size - extra), length, 0)
        return mine, theirs

    def join_rows(self, mine, theirs):
        return jnp.where(
            self.half == 0,
            jnp.concatenate([mine, theirs], axis=0),
            jnp.concatenate([theirs, mine], axis=0),
        )

    def outer_rows(self, value, extra):
        length = value.shape[0]
        edge = jnp.where(self.half == 0, value[:extra], value[length - extra :])
        return self.flip(edge, 1)

    def with_outer(self, value, extra):
        outer = self.outer_rows(value, extra)
        return jnp.where(
            self.half == 0,
            jnp.concatenate([outer, value], axis=0),
            jnp.concatenate([value, outer], axis=0),
        )

    def halo(self, value, first_row, last_row, flipped):
        pole = jnp.where(self.strip == 0, value[first_row], value[last_row])
        count = value.shape[0]
        ahead = self.to_prev(jnp.concatenate([value[:, 0], pole], axis=0))
        left = self.to_next(value[:, -1])
        pole = jnp.where(flipped, ahead[count:][::-1], ahead[count:])
        return left, ahead[:count], pole

    def halo_back(self, grad, rows, flipped):
        breadth = grad.shape[1]
        left, right = grad[rows + 4, : rows + 2], grad[rows + 7, : rows + 2]
        pole = jnp.where(self.strip == 0, grad[0], grad[rows + 1])
        corner = jnp.where(self.strip == 0, 0, rows + 1)
        inner = jnp.where(self.strip == 0, 1, rows)
        index = jnp.arange(rows + 2)[:, None]
        corners = []
        for name in range(2):
            rim = (left, right)[name]
            value = jnp.sum(jnp.where(index == corner, rim, 0.0), axis=0, keepdims=True)
            corners.append(0.5 * value * jnp.where(self.at_pole, 1.0, 0.0))
        left = left + jnp.where(index == inner, corners[0], 0.0)
        right = right + jnp.where(index == inner, corners[1], 0.0)
        column = jnp.arange(breadth)[:, None]
        pole = pole + jnp.where(column == 0, corners[0], 0.0)
        pole = pole + jnp.where(column == breadth - 1, corners[1], 0.0)
        pole = jnp.where(flipped, pole[::-1], pole)
        behind = self.to_next(jnp.concatenate([right, pole], axis=0))
        add_last = self.to_prev(left)
        add_pole = jnp.where(self.at_pole, behind[rows + 2 :], 0.0)
        return behind[: rows + 2], add_last, add_pole


def masked_stats(place, sea_weight, features):
    count = jnp.sum(sea_weight)
    mean = jnp.sum(sea_weight * features, axis=(0, 1)) / jnp.maximum(count, 1.0)
    centred = features - mean
    spread = jnp.sum(sea_weight * centred * centred, axis=(0, 1))
    state = jnp.stack([jnp.full_like(mean, count), mean, spread])
    for bit in place.bits():
        first, second = place.ordered(state, place.flip(state, bit), bit)
        total = first[0] + second[0]
        safe = jnp.maximum(total, 1.0)
        step = second[1] - first[1]
        state = jnp.stack(
            [
                total,
                (first[0] * first[1] + second[0] * second[1]) / safe,
                first[2] + second[2] + step * step * (first[0] * second[0] / safe),
            ]
        )
    return state[0], state[1], state[2] / state[0]


def bits_of(value):
    high = lax.reduce_precision(value, 8, 7)
    return high.astype(BF16), (value - high).astype(BF16)


def local(
    mesh, features, sea_mask, edge_flip, w_first, b_first, w_second, b_second, w_skip, b_skip,
    run_mean, run_var, cotangent,
):
    rows, breadth, own = features.shape
    place = Place(mesh, rows, breadth)
    size, depth = rows // 2, 2 * own
    flags = jnp.stack([place.at_top, place.at_bottom, place.side == 1]).astype(jnp.int32)
    flip_row = jnp.sum(jnp.where((jnp.arange(4) == place.ribbon)[:, None], edge_flip, 0), axis=0)
    flipped = jnp.where(place.strip == 0, flip_row[0], flip_row[1]) == 1

    packed = jnp.concatenate(
        [
            w_first.reshape(-1, own),
            w_second.reshape(-1, own),
            w_skip,
            b_first[None],
            b_second[None],
            b_skip[None],
        ],
        axis=0,
    )
    unit = 8 * place.count
    packed = jnp.pad(packed, ((0, -packed.shape[0] % unit), (0, 0)))
    share = packed.shape[0] // place.count
    other = place.across(lax.dynamic_slice_in_dim(packed, place.pix * share, share, 0))
    other = place.gathered(other)
    full = jnp.concatenate([packed, other], axis=1)

    def swapped(weights):
        return jnp.where(place.side == 0, weights, jnp.roll(weights, own, axis=-2))

    taps = 9 * depth
    first_full = swapped(full[:taps].reshape(3, 3, depth, depth))
    second_full = swapped(full[taps : 2 * taps].reshape(3, 3, depth, depth))
    skip_full = swapped(full[2 * taps : 2 * taps + depth])
    biases = full[2 * taps + depth : 2 * taps + depth + 3]

    def forward_weights(weights):
        return bits_of(weights.reshape(3, 3 * depth, depth))

    def backward_weights(weights):
        return bits_of(weights[::-1, ::-1].transpose(0, 1, 3, 2).reshape(3, 3 * depth, depth))

    mine, theirs = place.halves(features, 4, size)
    got = place.across(theirs)
    cot_mine, cot_theirs = place.halves(cotangent, 2, size)
    cot_got = place.across(cot_theirs)

    sea_weight = sea_mask.astype(F32)[:, :, None]
    sea_count, batch_mean, batch_var = masked_stats(place, sea_weight, features)
    inverse = lax.rsqrt(batch_var + EPSILON)
    moments = jnp.stack([batch_mean, inverse])
    moments = jnp.concatenate([moments, place.across(moments)], axis=1)

    weight_mine, _ = place.halves(sea_weight, 4, size)
    scaled = weight_mine * (jnp.concatenate([mine, got], axis=2) - moments[0]) * moments[1]
    scaled = place.with_outer(scaled, 4)
    x_left, x_right, x_pole = place.halo(scaled, 4, size + 3, flipped)

    def shift_scratch(blocks):
        return [pltpu.VMEM((blocks * breadth, 3 * depth), BF16) for _ in range(2)]

    def edges():
        return [pltpu.VMEM((breadth + 8, depth), F32) for _ in range(2)]

    def turned():
        return [pltpu.VMEM((depth, size * breadth), BF16) for _ in range(2)]

    hidden, slope_first = call(
        functools.partial(first_kernel, tile=9),
        [(size + 6, breadth, depth)] * 2,
        shift_scratch(size + 8),
        flags, scaled, x_left, x_right, x_pole, *forward_weights(first_full), biases[0:1],
    )
    h_left, h_right, h_pole = place.halo(hidden, 3, size + 2, flipped)
    out_rows, slope_second = call(
        functools.partial(second_kernel, tile=13),
        [(size + 4, breadth, depth)] * 2,
        shift_scratch(size + 6),
        flags, hidden, h_left, h_right, h_pole, *forward_weights(second_full), biases[1:2],
        scaled, *bits_of(skip_full), biases[2:3],
    )
    out_rows = out_rows[2 : size + 2]
    output = place.join_rows(out_rows[:, :, :own], place.across(out_rows[:, :, own:]))

    cot = place.with_outer(jnp.concatenate([cot_mine, cot_got], axis=2), 2)
    upper, grad_second = call(
        functools.partial(back_second_kernel, tile=8),
        [(size + 8, breadth, depth), (size, breadth, depth)],
        shift_scratch(size + 10) + edges(),
        flags, cot, slope_second, *backward_weights(second_full),
    )
    add_first, add_last, add_pole = place.halo_back(upper, size, flipped)
    gw_second, gb_second = call(
        functools.partial(weight_kernel, begin=2, top=2, bottom=size + 3, skip=False),
        [(3, 3, depth, depth), (1, depth)],
        shift_scratch(size + 2) + turned(),
        flags, hidden, h_left, h_right, h_pole, grad_second,
    )
    lower, grad_first = call(
        functools.partial(back_first_kernel, tile=8),
        [(size + 8, breadth, depth), (size, breadth, depth)],
        shift_scratch(size + 10) + edges(),
        flags, upper, add_first, add_last, add_pole, slope_first, cot,
        *backward_weights(first_full), *bits_of(skip_full.T),
    )
    add_first, add_last, add_pole = place.halo_back(lower, size, flipped)
    gw_first, gb_first, gw_skip, gb_skip = call(
        functools.partial(weight_kernel, begin=3, top=3, bottom=size + 4, skip=True),
        [(3, 3, depth, depth), (1, depth), (depth, depth), (1, depth)],
        shift_scratch(size + 2) + turned(),
        flags, scaled, x_left, x_right, x_pole, grad_first, cot,
    )

    column = jnp.arange(breadth)[None, :, None]
    row = jnp.arange(size)[:, None, None]
    edge = jnp.where(place.strip == 0, 0, size - 1)
    grad_in = lower[1 : size + 1]
    grad_in = grad_in + jnp.where(column == 0, add_first[1 : size + 1, None], 0.0)
    grad_in = grad_in + jnp.where(column == breadth - 1, add_last[1 : size + 1, None], 0.0)
    grad_in = grad_in + jnp.where(row == edge, add_pole[None], 0.0)
    own_weight = lax.dynamic_slice_in_dim(sea_weight, place.half * size, size, 0)
    first_sum = jnp.sum(own_weight * grad_in, axis=(0, 1))
    second_sum = jnp.sum(scaled[4 : size + 4] * grad_in, axis=(0, 1))
    sums = jnp.concatenate(
        [gb_first, gb_second, gb_skip, first_sum[None], second_sum[None]], axis=0
    )
    sums = place.summed(sums)
    sums = sums[:, :own] + place.across(sums[:, own:])
    grad_in = place.join_rows(grad_in[:, :, :own], place.across(grad_in[:, :, own:]))
    normed = (features - batch_mean) * inverse
    grad_features = (
        sea_weight * inverse * (grad_in - sums[3] / sea_count - normed * sums[4] / sea_count)
    )

    def all_summed(grad):
        part = place.reduced(grad)
        part = part[:, :own] + place.across(part[:, own:])
        return place.spread(part)

    gw_second = all_summed(
        jnp.concatenate([gw_second.reshape(taps, depth), gw_skip], axis=0)
    )
    gw_first = all_summed(gw_first.reshape(taps, depth))
    new_mean = (1.0 - MOMENTUM) * run_mean + MOMENTUM * batch_mean
    new_var = (1.0 - MOMENTUM) * run_var + MOMENTUM * batch_var * sea_count / (sea_count - 1.0)
    return (
        output,
        grad_features,
        gw_first.reshape(3, 3, depth, own),
        sums[0],
        gw_second[:taps].reshape(3, 3, depth, own),
        sums[1],
        gw_second[taps:],
        sums[2],
        new_mean,
        new_var,
    )


def solution(mesh):
    field, kernel, vector = P("pix", None, "ch"), P(None, None, None, "ch"), P("ch")
    placed = (
        field, P("pix", None), P(), kernel, vector, kernel, vector, P(None, "ch"), vector,
        vector, vector, field,
    )
    return jax.shard_map(
        functools.partial(local, mesh),
        mesh=mesh,
        in_specs=placed,
        out_specs=(
            field, field, kernel, vector, kernel, vector, P(None, "ch"), vector, vector, vector,
        ),
        check_vma=False,
    )
```

time: 1740 us -> 499 us (0.29); the launches traced: 1720 us -> 495 us
  matrix products: 615 us -> 0 us
  local copies, waits for them, and re-layouts: 554 us -> 83.3 us
  waiting for transfers between devices: 299 us -> 135 us
  Pallas kernels: 0 us -> 138 us
  blocking collectives: 98.8 us -> 0 us
  starting transfers between devices: 41.3 us -> 63 us
  other arithmetic: 92.6 us -> 72.1 us
    dot_general x57 -> x0, matrix products: 615 us -> none  [the longest x18 207 us: tap_grads(): jnp.einsum('hwi,hwo->io', padded[row_tap:row_tap + height, col_tap:col_ta...]
    scatter-add x36 -> x0, local copies, waits for them, and re-layouts: 446 us -> none  [the longest x14 375 us: conv_back(): summed.at[row_tap:row_tap + height, col_tap:col_tap + breadth].add(contrib)]
    all_gather x2 -> x0, waiting for transfers between devices: 153 us -> none  [padded_full(): return pad_faces(lax.all_gather(values, 'ch', axis=2, tiled=True), placing)]
    pallas_call x0 -> x6, Pallas kernels: none -> 138 us  [call(): pl.pallas_call(kernel, out_shape=[jax.ShapeDtypeStruct(shape, F32) for sh...]
    ppermute x24 -> x47, waiting for transfers between devices: 16.7 us -> 135 us  [the longest x30 70.1 us: flip(): return lax.ppermute(value, 'pix', [(i, i ^ bit) for i in range(self.count)])]
    psum x3 -> x0, blocking collectives: 98.8 us -> none  [the longest x1 35.6 us: masked_stats(): lax.psum((jnp.sum(sea_weight), jnp.sum(sea_weight * features, axis=(0, 1)...]
    reduce_scatter x2 -> x0, waiting for transfers between devices: 76.5 us -> none  [owned_grad(): lax.psum_scatter(unpad_faces(grad, placing), 'ch', scatter_dimension=2, t...]
    slice x18 -> x23, local copies, waits for them, and re-layouts: 70.6 us -> 17.6 us  [the longest x1 3.11 us: local(): first_full = swapped(full[:taps].reshape(3, 3, depth, depth))]
  transfers between devices with their start and end apart: 29 -> 47, of which waited for: 10 -> 25; matrix products, arithmetic and copies ran while one was open for 22% -> 19% of each run, Pallas kernels for 0% -> 9%
where the time goes in v1:
time: 499 us; the launch traced here: 495 us
  Pallas kernels  138 us (28%)
  waiting for transfers between devices  135 us (27%)
  local copies, waits for them, and re-layouts  83.3 us (17%)
  other arithmetic  72.1 us (14%)
  starting transfers between devices  63 us (13%)
    pallas_call x6, Pallas kernels, call(): pl.pallas_call(kernel, out_shape=[jax.ShapeDtypeStruct(shape, F32) for sh...  138 us
    ppermute x30, waiting for transfers between devices, flip(): return lax.ppermute(value, 'pix', [(i, i ^ bit) for i in range(self.count)])  70.1 us
    ppermute x9, waiting for transfers between devices, across(): return lax.ppermute(value, 'ch', [(0, 1), (1, 0)])  60.7 us
    ppermute x30, starting transfers between devices, flip(): return lax.ppermute(value, 'pix', [(i, i ^ bit) for i in range(self.count)])  31.6 us
    ppermute x4, starting transfers between devices, to_prev(): return lax.ppermute(value, 'pix', self.ribbon_pairs(-1))  20.1 us
    convert_element_type x7, other arithmetic, bits_of(): return (high.astype(BF16), (value - high).astype(BF16))  12.4 us
    transpose x4, local copies, waits for them, and re-layouts, backward_weights(): weights[::-1, ::-1].transpose(0, 1, 3, 2).reshape(3, 3 * depth, depth)  11 us
  transfers between devices with their start and end apart: 47, of which 25 were waited for; matrix products, arithmetic and copies ran while one was open for 19% of the time, Pallas kernels for 9%

profile of v1, /device:TPU:0, one launch (start us, length us, event | category | flops | bytes accessed | tf_op | source)
XLA Modules:
  0.0 495.5 jit_solution(10567961857568751200)
XLA Ops:
  15.6 3.6 concatenate.101
  22.9 4.1 constant_dynamic-slice_fusion.2
  44.7 8.7 %collective-permute-done.10 = f32[312,128]{0,1:T(8,128)S(1)} collective-permute-done((f32[312,128]{0,1:T(8,128)}, f32[312,128]{0,1:T(8,128)S(1)}, u32[]{:S(2)}, u32[]{:S(2)}) %collective-permute-start.10) | collective-permute-done | bytes 159776 | tf_op jit(solution)/shard_map/ppermute | solution.py:280
  55.7 8.9 %collective-permute-done.11 = f32[2,312,128]{1,2,0:T(8,128)S(1)} collective-permute-done((f32[2,312,128]{1,2,0:T(8,128)S(1)}, f32[2,312,128]{1,2,0:T(8,128)S(1)}, u32[]{:S(2)}, u32[]{:S(2)}) %collective-permute-start.11) | collective-permute-done | bytes 319520 | tf_op jit(solution)/shard_map/ppermute | solution.py:280
  71.9 29.9 %collective-permute-done.5 = f32[2,128]{1,0:T(2,128)S(1)} collective-permute-done((f32[2,128]{1,0:T(2,128)S(1)}, f32[2,128]{1,0:T(2,128)S(1)}, u32[]{:S(2)}, u32[]{:S(2)}) %collective-permute-start.5) | collective-permute-done | bytes 1056 | tf_op jit(solution)/shard_map/ppermute | solution.py:277
  121.1 4.2 maximum_select_fusion.1.cot.rest_0_
  157.0 22.0 %shard_map.195 = (f32[54,64,256]{2,1,0:T(8,128)}, f32[54,64,256]{2,1,0:T(8,128)}) custom-call(s32[3]{0:T(128)} %add_convert_fusion.flags, f32[56,64,256]{2,1,0:T(8,128)} %copy-done, f32[56,256]{1,0:T(8,128)} %collective-permute-done.7.left, f32[56,256]{1,0:T(8,128)} %slice.465.right, f32[64,256]{1,0:T(8,128)} %broadcast_select_fusion.21.pole, ...), custom_call_target="tpu_custom_call" | custom-call | tf_op jit(solution)/shard_map/pallas_call | solution.py:238
  179.9 5.9 %copy.88 = f32[54,64,256]{2,0,1:T(8,128)} copy(f32[54,64,256]{2,1,0:T(8,128)} %get-tuple-element.24.x) | data formatting | bytes 7077888 | tf_op jit(solution)/shard_map/pallas_call | solution.py:238
  195.1 3.7 fusion.10
  205.4 3.5 fusion.9
  222.5 3.7 collective-permute-done.14.left
  226.8 23.6 %shard_map.196 = (f32[52,64,256]{2,1,0:T(8,128)}, f32[52,64,256]{2,1,0:T(8,128)}) custom-call(s32[3]{0:T(128)} %add_convert_fusion.flags, f32[54,64,256]{2,1,0:T(8,128)} %get-tuple-element.24.x, f32[54,256]{1,0:T(8,128)} %copy-done.22, f32[54,256]{1,0:T(8,128)} %slice.475.right, f32[64,256]{1,0:T(8,128)} %broadcast_select_fusion.20.pole, ...), custom_call_target="tpu_custom_call" | custom-call | tf_op jit(solution)/shard_map/pallas_call | solution.py:238
  250.4 22.3 %shard_map.197 = (f32[56,64,256]{2,1,0:T(8,128)}, f32[48,64,256]{2,1,0:T(8,128)}) custom-call(s32[3]{0:T(128)} %add_convert_fusion.flags, f32[52,64,256]{2,1,0:T(8,128)} %maximum_select_fusion.1.cot.rest_0_, f32[52,64,256]{2,1,0:T(8,128)} %get-tuple-element.26.slope, bf16[3,768,256]{2,1,0:T(8,128)(2,1)} %get-tuple-element.93.w_high, ...), custom_call_target="tpu_custom_call" | custom-call | tf_op jit(solution)/shard_map/pallas_call | solution.py:238
  277.3 14.5 %collective-permute-start.20 = (f32[50,256]{1,0:T(8,128)S(1)}, f32[50,256]{1,0:T(8,128)S(1)}, u32[]{:S(2)}, u32[]{:S(2)}) collective-permute-start(f32[50,256]{1,0:T(8,128)S(1)} %get-tuple-element.72), channel_id=1, source_target_pairs={{0,12},{2,14},{4,0},{6,2},{8,4},{10,6},{12,8},{14,10},{16,28},{18,... | collective-permute-start | bytes 153608 | tf_op jit(solution)/shard_map/ppermute | solution.py:274
  294.4 26.6 %shard_map.198 = (f32[56,64,256]{2,1,0:T(8,128)}, f32[48,64,256]{2,1,0:T(8,128)}) custom-call(s32[3]{0:T(128)} %add_convert_fusion.flags, f32[56,64,256]{2,1,0:T(8,128)} %get-tuple-element.27.upper, f32[50,256]{1,0:T(8,128)} %slice.489.add_first, f32[50,256]{1,0:T(8,128)} %copy-done.24, f32[64,256]{1,0:T(8,128)} %slice_select_fusion.10.add_pole, ...), custom_call_target="tpu_custom_call" | custom-call | tf_op jit(solution)/shard_map/pallas_call | solution.py:238
  328.2 19.9 %shard_map.200 = (f32[3,3,256,256]{3,2,1,0:T(8,128)}, f32[1,256]{1,0:T(1,128)}) custom-call(s32[3]{0:T(128)} %add_convert_fusion.flags, f32[54,64,256]{2,1,0:T(8,128)} %get-tuple-element.24.x, f32[54,256]{1,0:T(8,128)} %copy-done.22, f32[54,256]{1,0:T(8,128)} %slice.475.right, f32[64,256]{1,0:T(8,128)} %broadcast_select_fusion.20.pole, ...), custom_call_target="tpu_custom_call" | custom-call | tf_op jit(solution)/shard_map/pallas_call | solution.py:238
  348.2 23.6 %shard_map.199 = (f32[3,3,256,256]{3,2,1,0:T(8,128)}, f32[1,256]{1,0:T(1,128)}, f32[256,256]{1,0:T(8,128)}, f32[1,256]{1,0:T(1,128)}) custom-call(s32[3]{0:T(128)} %add_convert_fusion.flags, f32[56,64,256]{2,1,0:T(8,128)} %copy-done, f32[56,256]{1,0:T(8,128)} %collective-permute-done.7.left, f32[56,256]{1,0:T(8,128)} %slice.465.right, ...), custom_call_target="tpu_custom_call" | custom-call | tf_op jit(solution)/shard_map/pallas_call | solution.py:238
  372.7 3.9 fusion.3
  393.2 26.2 %collective-permute-done.28 = f32[5,128]{1,0:T(8,128)S(1)} collective-permute-done((f32[5,128]{1,0:T(8,128)S(1)}, f32[5,128]{1,0:T(8,128)S(1)}, u32[]{:S(2)}, u32[]{:S(2)}) %collective-permute-start.28) | collective-permute-done | bytes 2592 | tf_op jit(solution)/shard_map/ppermute | solution.py:277
  422.8 13.8 %collective-permute-done.30 = f32[576,256]{1,0:T(8,128)S(1)} collective-permute-done((f32[576,256]{1,0:T(8,128)S(1)}, f32[576,256]{1,0:T(8,128)S(1)}, u32[]{:S(2)}, u32[]{:S(2)}) %collective-permute-start.30) | collective-permute-done | bytes 589856 | tf_op jit(solution)/shard_map/ppermute | solution.py:280
  437.6 10.0 %collective-permute-done.39 = f32[640,256]{1,0:T(8,128)S(1)} collective-permute-done((f32[640,256]{1,0:T(8,128)S(1)}, f32[640,256]{1,0:T(8,128)S(1)}, u32[]{:S(2)}, u32[]{:S(2)}) %collective-permute-start.39) | collective-permute-done | bytes 655392 | tf_op jit(solution)/shard_map/ppermute | solution.py:280
  464.1 3.5 collective-permute-done.41
  468.4 3.8 collective-permute-done.42
  487.5 3.6 fusion.6
  (352 shorter events, 198.1 us)
Async XLA Ops:
  8.5 23.4 %collective-permute-start.1 = (f32[3,128]{1,0:T(4,128)}, f32[3,128]{1,0:T(4,128)}, u32[]{:S(2)}, u32[]{:S(2)}) collective-permute-start(f32[3,128]{1,0:T(4,128)} %pad_maximum_fusion.20), channel_id=1, source_target_pairs={{0,2},{2,0},{4,6},{6,4},{8,10},{10,8},{12,14},{14,12},{16,18},{18,... | collective-permute-start | bytes 4616 | tf_op jit(solution)/shard_map/ppermute | solution.py:280
  20.4 23.0 %collective-permute-start.9 = (f32[312,128]{0,1:T(8,128)S(1)}, f32[312,128]{0,1:T(8,128)}, u32[]{:S(2)}, u32[]{:S(2)}) collective-permute-start(f32[312,128]{0,1:T(8,128)S(1)} %constant_dynamic-slice_fusion.3), channel_id=1, source_target_pairs={{0,1},{1,0},{2,3},{3,2},{4,5},{5,4},{6,7},{7,6},{8,9},{9,8},{10,11... | collective-permute-start | bytes 479240 | tf_op jit(solution)/shard_map/ppermute | solution.py:277
  27.0 88.0 %collective-permute-start.17 = (f32[50,64,128]{2,1,0:T(8,128)}, f32[50,64,128]{2,1,0:T(8,128)}, u32[]{:S(2)}, u32[]{:S(2)}) collective-permute-start(f32[50,64,128]{2,1,0:T(8,128)} %get-tuple-element.83), channel_id=1, source_target_pairs={{0,1},{1,0},{2,3},{3,2},{4,5},{5,4},{6,7},{7,6},{8,9},{9,8},{10,11... | collective-permute-start | bytes 4915208 | tf_op jit(solution)/shard_map/ppermute | solution.py:277
  29.1 76.5 %collective-permute-start = (f32[52,64,128]{2,1,0:T(8,128)}, f32[52,64,128]{2,1,0:T(8,128)}, u32[]{:S(2)}, u32[]{:S(2)}) collective-permute-start(f32[52,64,128]{2,1,0:T(8,128)} %get-tuple-element.87), channel_id=1, source_target_pairs={{0,1},{1,0},{2,3},{3,2},{4,5},{5,4},{6,7},{7,6},{8,9},{9,8},{10,11... | collective-permute-start | bytes 5111816 | tf_op jit(solution)/shard_map/ppermute | solution.py:277
  43.4 10.0 %collective-permute-start.10 = (f32[312,128]{0,1:T(8,128)}, f32[312,128]{0,1:T(8,128)S(1)}, u32[]{:S(2)}, u32[]{:S(2)}) collective-permute-start(f32[312,128]{0,1:T(8,128)} %collective-permute-done.9), channel_id=1, source_target_pairs={{0,16},{2,18},{4,20},{6,22},{8,24},{10,26},{12,28},{14,30},{16,0},... | collective-permute-start | bytes 479240 | tf_op jit(solution)/shard_map/ppermute | solution.py:280
  54.4 10.1 %collective-permute-start.11 = (f32[2,312,128]{1,2,0:T(8,128)S(1)}, f32[2,312,128]{1,2,0:T(8,128)S(1)}, u32[]{:S(2)}, u32[]{:S(2)}) collective-permute-start(f32[2,312,128]{1,2,0:T(8,128)S(1)} %pad_maximum_fusion.9), channel_id=1, source_target_pairs={{0,8},{2,10},{4,12},{6,14},{8,0},{10,2},{12,4},{14,6},{16,24},{18,... | collective-permute-start | bytes 958472 | tf_op jit(solution)/shard_map/ppermute | solution.py:280
  65.8 36.0 %collective-permute-start.12 = (f32[2,2,312,128]{3,2,1,0:T(8,128)S(1)}, f32[2,2,312,128]{3,2,1,0:T(8,128)}, u32[]{:S(2)}, u32[]{:S(2)}) collective-permute-start(f32[2,2,312,128]{3,2,1,0:T(8,128)S(1)} %copy.77), channel_id=1, source_target_pairs={{0,4},{2,6},{4,0},{6,2},{8,12},{10,14},{12,8},{14,10},{16,20},{18,... | collective-permute-start | bytes 1916936 | tf_op jit(solution)/shard_map/ppermute | solution.py:280
  67.4 34.4 %collective-permute-start.5 = (f32[2,128]{1,0:T(2,128)S(1)}, f32[2,128]{1,0:T(2,128)S(1)}, u32[]{:S(2)}, u32[]{:S(2)}) collective-permute-start(f32[2,128]{1,0:T(2,128)S(1)} %pad_maximum_fusion.25), channel_id=1, source_target_pairs={{0,1},{1,0},{2,3},{3,2},{4,5},{5,4},{6,7},{7,6},{8,9},{9,8},{10,11... | collective-permute-start | bytes 3080 | tf_op jit(solution)/shard_map/ppermute | solution.py:277
  114.6 14.6 %collective-permute-start.13 = (f32[2,2,2,312,128]{4,3,2,1,0:T(8,128)}, f32[2,2,2,312,128]{4,3,2,1,0:T(8,128)}, u32[]{:S(2)}, u32[]{:S(2)}) collective-permute-start(f32[2,2,2,312,128]{4,3,2,1,0:T(8,128)} %copy.80), channel_id=1, source_target_pairs={{0,2},{2,0},{4,6},{6,4},{8,10},{10,8},{12,14},{14,12},{16,18},{18,... | collective-permute-start | bytes 3833864 | tf_op jit(solution)/shard_map/ppermute | solution.py:280
  125.9 31.2 %collective-permute-start.7 = (f32[56,256]{1,0:T(8,128)}, f32[56,256]{1,0:T(8,128)}, u32[]{:S(2)}, u32[]{:S(2)}) collective-permute-start(f32[56,256]{1,0:T(8,128)} %bitcast.152), channel_id=1, source_target_pairs={{0,4},{2,6},{4,8},{6,10},{8,12},{10,14},{12,0},{14,2},{16,20},{18,... | collective-permute-start | bytes 172040 | tf_op jit(solution)/shard_map/ppermute | solution.py:271
  211.1 10.1 %collective-permute-start.15 = (f32[118,256]{1,0:T(8,128)}, f32[118,256]{1,0:T(8,128)S(1)}, u32[]{:S(2)}, u32[]{:S(2)}) collective-permute-start(f32[118,256]{1,0:T(8,128)} %pad_maximum_fusion.17), channel_id=1, source_target_pairs={{0,12},{2,14},{4,0},{6,2},{8,4},{10,6},{12,8},{14,10},{16,28},{18,... | collective-permute-start | bytes 362504 | tf_op jit(solution)/shard_map/ppermute | solution.py:274
  276.6 15.2 %collective-permute-start.19 = (f32[114,256]{1,0:T(8,128)S(1)}, f32[114,256]{1,0:T(8,128)S(1)}, u32[]{:S(2)}, u32[]{:S(2)}) collective-permute-start(f32[114,256]{1,0:T(8,128)S(1)} %pad_maximum_fusion.18), channel_id=1, source_target_pairs={{0,4},{2,6},{4,8},{6,10},{8,12},{10,14},{12,0},{14,2},{16,20},{18,... | collective-permute-start | bytes 350216 | tf_op jit(solution)/shard_map/ppermute | solution.py:271
  277.3 16.4 %collective-permute-start.20 = (f32[50,256]{1,0:T(8,128)S(1)}, f32[50,256]{1,0:T(8,128)S(1)}, u32[]{:S(2)}, u32[]{:S(2)}) collective-permute-start(f32[50,256]{1,0:T(8,128)S(1)} %get-tuple-element.72), channel_id=1, source_target_pairs={{0,12},{2,14},{4,0},{6,2},{8,4},{10,6},{12,8},{14,10},{16,28},{18,... | collective-permute-start | bytes 153608 | tf_op jit(solution)/shard_map/ppermute | solution.py:274
  324.9 47.7 %collective-permute-start.21 = (f32[114,256]{1,0:T(8,128)S(1)}, f32[114,256]{1,0:T(8,128)S(1)}, u32[]{:S(2)}, u32[]{:S(2)}) collective-permute-start(f32[114,256]{1,0:T(8,128)S(1)} %pad_maximum_fusion.19), channel_id=1, source_target_pairs={{0,4},{2,6},{4,8},{6,10},{8,12},{10,14},{12,0},{14,2},{16,20},{18,... | collective-permute-start | bytes 350216 | tf_op jit(solution)/shard_map/ppermute | solution.py:271
  328.0 43.8 %collective-permute-start.22 = (f32[50,256]{1,0:T(8,128)S(1)}, f32[50,256]{1,0:T(8,128)}, u32[]{:S(2)}, u32[]{:S(2)}) collective-permute-start(f32[50,256]{1,0:T(8,128)S(1)} %get-tuple-element.70), channel_id=1, source_target_pairs={{0,12},{2,14},{4,0},{6,2},{8,4},{10,6},{12,8},{14,10},{16,28},{18,... | collective-permute-start | bytes 153608 | tf_op jit(solution)/shard_map/ppermute | solution.py:274
  382.0 69.3 %collective-permute-start.16 = (f32[48,64,128]{2,1,0:T(8,128)S(1)}, f32[48,64,128]{2,1,0:T(8,128)S(1)}, u32[]{:S(2)}, u32[]{:S(2)}) collective-permute-start(f32[48,64,128]{2,1,0:T(8,128)S(1)} %get-tuple-element.79), channel_id=1, source_target_pairs={{0,1},{1,0},{2,3},{3,2},{4,5},{5,4},{6,7},{7,6},{8,9},{9,8},{10,11... | collective-permute-start | bytes 4718600 | tf_op jit(solution)/shard_map/ppermute | solution.py:277
  383.4 36.6 %collective-permute-start.29 = (f32[1152,256]{1,0:T(8,128)S(1)}, f32[1152,256]{1,0:T(8,128)S(1)}, u32[]{:S(2)}, u32[]{:S(2)}) collective-permute-start(f32[1152,256]{1,0:T(8,128)S(1)} %slice_select_fusion.1), channel_id=1, source_target_pairs={{0,2},{2,0},{4,6},{6,4},{8,10},{10,8},{12,14},{14,12},{16,18},{18,... | collective-permute-start | bytes 3538952 | tf_op jit(solution)/shard_map/ppermute | solution.py:280
  388.9 31.7 %collective-permute-start.38 = (f32[1280,256]{1,0:T(8,128)S(1)}, f32[1280,256]{1,0:T(8,128)S(1)}, u32[]{:S(2)}, u32[]{:S(2)}) collective-permute-start(f32[1280,256]{1,0:T(8,128)S(1)} %slice_select_fusion), channel_id=1, source_target_pairs={{0,2},{2,0},{4,6},{6,4},{8,10},{10,8},{12,14},{14,12},{16,18},{18,... | collective-permute-start | bytes 3932168 | tf_op jit(solution)/shard_map/ppermute | solution.py:280
  390.7 28.8 %collective-permute-start.28 = (f32[5,128]{1,0:T(8,128)S(1)}, f32[5,128]{1,0:T(8,128)S(1)}, u32[]{:S(2)}, u32[]{:S(2)}) collective-permute-start(f32[5,128]{1,0:T(8,128)S(1)} %slice.498), channel_id=1, source_target_pairs={{0,1},{1,0},{2,3},{3,2},{4,5},{5,4},{6,7},{7,6},{8,9},{9,8},{10,11... | collective-permute-start | bytes 7688 | tf_op jit(solution)/shard_map/ppermute | solution.py:277
  392.8 94.7 %collective-permute-start.23 = (f32[48,64,128]{2,1,0:T(8,128)S(1)}, f32[48,64,128]{2,1,0:T(8,128)S(1)}, u32[]{:S(2)}, u32[]{:S(2)}) collective-permute-start(f32[48,64,128]{2,1,0:T(8,128)S(1)} %get-tuple-element.81), channel_id=1, source_target_pairs={{0,1},{1,0},{2,3},{3,2},{4,5},{5,4},{6,7},{7,6},{8,9},{9,8},{10,11... | collective-permute-start | bytes 4718600 | tf_op jit(solution)/shard_map/ppermute | solution.py:277
  420.3 16.3 %collective-permute-start.30 = (f32[576,256]{1,0:T(8,128)S(1)}, f32[576,256]{1,0:T(8,128)S(1)}, u32[]{:S(2)}, u32[]{:S(2)}) collective-permute-start(f32[576,256]{1,0:T(8,128)S(1)} %slice_select_fusion.3), channel_id=1, source_target_pairs={{0,4},{2,6},{4,0},{6,2},{8,12},{10,14},{12,8},{14,10},{16,20},{18,... | collective-permute-start | bytes 1769480 | tf_op jit(solution)/shard_map/ppermute | solution.py:280
  420.9 26.7 %collective-permute-start.39 = (f32[640,256]{1,0:T(8,128)S(1)}, f32[640,256]{1,0:T(8,128)S(1)}, u32[]{:S(2)}, u32[]{:S(2)}) collective-permute-start(f32[640,256]{1,0:T(8,128)S(1)} %slice_select_fusion.2), channel_id=1, source_target_pairs={{0,4},{2,6},{4,0},{6,2},{8,12},{10,14},{12,8},{14,10},{16,20},{18,... | collective-permute-start | bytes 1966088 | tf_op jit(solution)/shard_map/ppermute | solution.py:280
  436.8 11.8 %collective-permute-start.31 = (f32[288,256]{1,0:T(8,128)S(1)}, f32[288,256]{1,0:T(8,128)S(1)}, u32[]{:S(2)}, u32[]{:S(2)}) collective-permute-start(f32[288,256]{1,0:T(8,128)S(1)} %slice_select_fusion.5), channel_id=1, source_target_pairs={{0,8},{2,10},{4,12},{6,14},{8,0},{10,2},{12,4},{14,6},{16,24},{18,... | collective-permute-start | bytes 884744 | tf_op jit(solution)/shard_map/ppermute | solution.py:280
  447.7 10.6 %collective-permute-start.40 = (f32[320,256]{1,0:T(8,128)S(1)}, f32[320,256]{1,0:T(8,128)S(1)}, u32[]{:S(2)}, u32[]{:S(2)}) collective-permute-start(f32[320,256]{1,0:T(8,128)S(1)} %slice_select_fusion.4), channel_id=1, source_target_pairs={{0,8},{2,10},{4,12},{6,14},{8,0},{10,2},{12,4},{14,6},{16,24},{18,... | collective-permute-start | bytes 983048 | tf_op jit(solution)/shard_map/ppermute | solution.py:280
  (69 other events, 416.1 us)

commit v2 on v1

v2 whole, which is shorter than its diff:
```python
import functools

import jax
import jax.numpy as jnp
from jax import lax
from jax.experimental import pallas as pl
from jax.experimental.pallas import tpu as pltpu
from jax.sharding import PartitionSpec as P

EPSILON = 1e-05
MOMENTUM = 0.1
INV_ROOT_TWO_PI = 0.3989422804014327
SQRT_HALF = 0.7071067811865476
F32 = jnp.float32
BF16 = jnp.bfloat16
VMEM_LIMIT = 60 * 1024 * 1024


def split(value):
    high = value.astype(BF16)
    return high, (value - high.astype(F32)).astype(BF16)


def dot_split(a_high, a_low, b_high, b_low):
    total = jnp.dot(a_high, b_high, preferred_element_type=F32)
    total = total + jnp.dot(a_high, b_low, preferred_element_type=F32)
    return total + jnp.dot(a_low, b_high, preferred_element_type=F32)


def gelu_and_slope(u):
    cdf = 0.5 * (1.0 + lax.erf(u * SQRT_HALF))
    return u * cdf, cdf + u * jnp.exp(-0.5 * u * u) * INV_ROOT_TWO_PI


def put_shifts(high, low, block, value, left, right):
    breadth, depth = value.shape
    column = lax.broadcasted_iota(jnp.int32, (breadth, 1), 0)
    shifts = (
        jnp.where(column == 0, left, pltpu.roll(value, 1, 0)),
        value,
        jnp.where(column == breadth - 1, right, pltpu.roll(value, breadth - 1, 0)),
    )
    for tap, piece in enumerate(shifts):
        piece_high, piece_low = split(piece)
        high[pl.ds(block * breadth, breadth), tap * depth : (tap + 1) * depth] = piece_high
        low[pl.ds(block * breadth, breadth), tap * depth : (tap + 1) * depth] = piece_low


def conv_rows(high, low, w_high, w_low, first, rows, breadth):
    total = None
    for row_tap in range(3):
        window = pl.ds(pl.multiple_of((first + row_tap) * breadth, breadth), rows * breadth)
        part = dot_split(high[window, :], low[window, :], w_high[row_tap], w_low[row_tap])
        total = part if total is None else total + part
    return total


AT_TOP, AT_BOTTOM, SIDE, HALF, FLIPPED, PIX = range(6)
NOT_SEA = 1e30


def put_padded(flags, x, left, ahead, pole, high, low, begin, count, top, bottom):
    rows, breadth = x.shape[0], x.shape[1]

    @pl.loop(0, count)
    def _(block):
        row = block + begin
        put_shifts(high, low, block, x[row], left[pl.ds(row, 1)], ahead[pl.ds(row, 1)])

    def put_pole(at, edge):
        @pl.when(flags[FLIPPED] == 1)
        def _():
            for column in range(breadth):
                pole[column : column + 1] = ahead[rows + breadth - 1 - column : rows + breadth - column]

        @pl.when(flags[FLIPPED] == 0)
        def _():
            pole[...] = ahead[rows : rows + breadth]

        corner_left = 0.5 * (pole[0:1] + left[edge : edge + 1])
        corner_right = 0.5 * (pole[breadth - 1 : breadth] + ahead[edge : edge + 1])
        put_shifts(high, low, at - begin, pole[...], corner_left, corner_right)

    @pl.when(flags[AT_TOP] == 1)
    def _():
        put_pole(top, top + 1)

    @pl.when(flags[AT_BOTTOM] == 1)
    def _():
        put_pole(bottom, bottom - 1)


def put_messages(flags, x, to_prev, to_next, first_row, last_row):
    rows, breadth = x.shape[0], x.shape[1]

    @pl.loop(0, rows)
    def _(row):
        to_prev[pl.ds(row, 1)] = x[row, 0:1]
        to_next[pl.ds(row, 1)] = x[row, breadth - 1 : breadth]

    to_prev[rows : rows + breadth] = x[jnp.where(flags[AT_BOTTOM] == 1, last_row, first_row)]


def first_kernel(
    flags, marked, got, halo_mine, halo_got, w_high, w_low, biases,
    scaled, x_left, x_ahead, hidden, slope, to_prev, to_next, pole, high, low, *, tile
):
    blocks, breadth, depth = scaled.shape
    own = depth // 2
    extra = blocks - got.shape[0]
    tail = halo_mine.shape[0] - 8
    start = flags[HALF] * (marked.shape[0] - got.shape[0])

    def normal(value, lanes):
        source = halo_mine if lanes.start == 0 else halo_got
        mean, inverse = source[tail : tail + 1], source[tail + 1 : tail + 2]
        return jnp.where(value > 0.1 * NOT_SEA, 0.0, (value - mean) * inverse)

    lower, upper = slice(0, own), slice(own, depth)
    main = jnp.where(flags[HALF] == 0, extra, 0)
    outer = jnp.where(flags[HALF] == 0, 0, blocks - extra)

    @pl.loop(0, got.shape[0])
    def _(row):
        scaled[main + row, :, lower] = normal(marked[start + row], lower)
        scaled[main + row, :, upper] = normal(got[row], upper)

    for row in range(extra):
        rows = slice(row * breadth, (row + 1) * breadth)
        scaled[outer + row, :, lower] = normal(halo_mine[rows], lower)
        scaled[outer + row, :, upper] = normal(halo_got[rows], upper)

    begin = extra * breadth
    for target, start, count in (
        (x_left, begin, blocks),
        (x_ahead, begin + blocks, blocks + breadth),
    ):
        rows = slice(start, start + count)
        target[:, lower] = normal(halo_mine[rows], lower)
        target[:, upper] = normal(halo_got[rows], upper)

    put_padded(flags, scaled, x_left, x_ahead, pole, high, low, 0, blocks, 3, blocks - 4)

    @pl.loop(0, (blocks - 2) // tile)
    def _(step):
        first = step * tile
        pre = conv_rows(high, low, w_high, w_low, first, tile, breadth) + biases[0:1]
        value, grad = gelu_and_slope(pre)
        hidden[pl.ds(first, tile)] = value.reshape(tile, breadth, depth)
        slope[pl.ds(first, tile)] = grad.reshape(tile, breadth, depth)

    put_messages(flags, hidden, to_prev, to_next, 3, blocks - 6)


def second_kernel(
    flags, x, left, ahead, w_high, w_low, biases, source, s_high, s_low,
    out_own, out_send, slope, pole, high, low, *, tile
):
    blocks, breadth, depth = x.shape
    own = depth // 2
    put_padded(flags, x, left, ahead, pole, high, low, 0, blocks, 2, blocks - 3)

    @pl.loop(0, (blocks - 2) // tile)
    def _(step):
        first = step * tile
        pre = conv_rows(high, low, w_high, w_low, first, tile, breadth) + biases[1:2]
        value, grad = gelu_and_slope(pre)
        slope[pl.ds(first, tile)] = grad.reshape(tile, breadth, depth)
        skip_high, skip_low = split(source[pl.ds(first + 2, tile)].reshape(tile * breadth, -1))
        skip = dot_split(skip_high, skip_low, s_high[...], s_low[...]) + biases[2:3]
        value = (value + skip).reshape(tile, breadth, depth)
        for block in range(tile):
            row = first + block - 2

            @pl.when((row >= 0) & (row < blocks - 6))
            def _():
                out_own[row] = value[block, :, :own]
                out_send[row] = value[block, :, own:]


def back_conv(flags, high, low, w_high, w_low, edge_first, edge_last, out, to_next, to_prev, blocks, breadth, tile):
    depth = edge_first.shape[1]
    for tap in range(3):
        for edge, slot, base in ((edge_first, 2, blocks), (edge_last, 0, blocks + 3)):
            rows = pl.ds((base + tap) * breadth, breadth)
            edge_high, edge_low = split(edge[tap : tap + breadth])
            zero = jnp.zeros((breadth, 3 * depth), BF16)
            high[rows, :] = zero
            low[rows, :] = zero
            high[rows, slot * depth : (slot + 1) * depth] = edge_high
            low[rows, slot * depth : (slot + 1) * depth] = edge_low

    @pl.loop(0, (blocks + 4) // tile)
    def _(step):
        first = step * tile
        out[pl.ds(first, tile)] = conv_rows(high, low, w_high, w_low, first, tile, breadth).reshape(
            tile, breadth, depth
        )

    count = blocks - 2
    to_prev[...] = out[blocks][:count]
    to_next[:count] = out[blocks + 3][:count]
    to_next[count:] = jnp.zeros((breadth, depth), F32)

    def put_pole(at, inner):
        corner_left = 0.5 * out[blocks][at : at + 1]
        corner_right = 0.5 * out[blocks + 3][at : at + 1]
        to_prev[inner : inner + 1] += corner_left
        to_next[inner : inner + 1] += corner_right
        column = lax.broadcasted_iota(jnp.int32, (breadth, 1), 0)
        row = out[at] + jnp.where(column == 0, corner_left, 0.0)
        row = row + jnp.where(column == breadth - 1, corner_right, 0.0)

        @pl.when(flags[FLIPPED] == 0)
        def _():
            to_next[count:] = row

        @pl.when(flags[FLIPPED] == 1)
        def _():
            for k in range(breadth):
                to_next[count + k : count + k + 1] = row[breadth - 1 - k : breadth - k]

    @pl.when(flags[AT_TOP] == 1)
    def _():
        put_pole(0, 1)

    @pl.when(flags[AT_BOTTOM] == 1)
    def _():
        put_pole(count - 1, count - 2)


def outside_pole(flags, block, blocks):
    return ((flags[AT_TOP] == 1) & (block < 2)) | ((flags[AT_BOTTOM] == 1) & (block >= blocks - 2))


def back_second_kernel(
    flags, cot_mine, cot_got, slope, w_high, w_low,
    out, grad, to_next, to_prev, high, low, edge_first, edge_last, *, tile
):
    blocks, breadth, depth = slope.shape
    edge_first[...] = jnp.zeros_like(edge_first)
    edge_last[...] = jnp.zeros_like(edge_last)

    @pl.loop(0, blocks)
    def _(block):
        outside = outside_pole(flags, block, blocks)
        value = jnp.concatenate([cot_mine[block], cot_got[block]], axis=1)
        value = value * slope[block] * jnp.where(outside, 0.0, 1.0)
        put_shifts(high, low, block, value, 0.0, 0.0)
        edge_first[pl.ds(block, 1)] = value[0:1]
        edge_last[pl.ds(block, 1)] = value[breadth - 1 : breadth]

        @pl.when((block >= 2) & (block < blocks - 2))
        def _():
            grad[block - 2] = value

    back_conv(
        flags, high, low, w_high, w_low, edge_first, edge_last, out, to_next, to_prev, blocks, breadth, tile
    )


def grad_first_kernel(flags, upper, behind, after, slope, grad):
    count, breadth, _ = grad.shape
    column = lax.broadcasted_iota(jnp.int32, (breadth, 1), 0)

    @pl.loop(0, count)
    def _(row):
        outside = ((flags[AT_TOP] == 1) & (row < 1)) | ((flags[AT_BOTTOM] == 1) & (row >= count - 1))
        edge = ((flags[AT_TOP] == 1) & (row == 1)) | ((flags[AT_BOTTOM] == 1) & (row == count - 2))
        value = upper[row] + jnp.where(column == 0, behind[pl.ds(row, 1)], 0.0)
        value = value + jnp.where(column == breadth - 1, after[pl.ds(row, 1)], 0.0)
        value = value + behind[count : count + breadth] * jnp.where(edge, 1.0, 0.0)
        grad[row] = value * slope[row + 2] * jnp.where(outside, 0.0, 1.0)


def back_first_kernel(
    flags, grad, cot_mine, cot_got, w_high, w_low, s_high, s_low,
    out_own, out_send, to_next, to_prev, out, high, low, edge_first, edge_last, *, tile
):
    blocks, breadth, own = cot_mine.shape
    depth = 2 * own
    edge_first[...] = jnp.zeros_like(edge_first)
    edge_last[...] = jnp.zeros_like(edge_last)
    none = jnp.zeros((breadth, depth), F32)
    put_shifts(high, low, 0, none, 0.0, 0.0)
    put_shifts(high, low, blocks - 1, none, 0.0, 0.0)

    @pl.loop(1, blocks - 1)
    def _(block):
        value = grad[block - 1]
        put_shifts(high, low, block, value, 0.0, 0.0)
        edge_first[pl.ds(block, 1)] = value[0:1]
        edge_last[pl.ds(block, 1)] = value[breadth - 1 : breadth]

    back_conv(
        flags, high, low, w_high, w_low, edge_first, edge_last, out, to_next, to_prev, blocks, breadth, tile
    )

    @pl.loop(0, (blocks - 4) // tile)
    def _(step):
        first = step * tile
        rows = pl.ds(first + 2, tile)
        cot = jnp.concatenate([cot_mine[rows], cot_got[rows]], axis=2).reshape(tile * breadth, depth)
        cot_high, cot_low = split(cot)
        skip = dot_split(cot_high, cot_low, s_high[...], s_low[...]).reshape(tile, breadth, depth)
        total = out[pl.ds(first + 1, tile)] + skip
        out_own[pl.ds(first, tile)] = total[:, :, :own]
        out_send[pl.ds(first, tile)] = total[:, :, own:]


def put_transposed(read, rows, breadth, high, low, total, tile):
    total[...] = jnp.zeros_like(total)

    @pl.loop(0, rows // tile)
    def _(step):
        piece = read(step * tile, tile)
        total[...] += jnp.sum(piece, axis=0, keepdims=True)
        piece_high, piece_low = split(piece.T)
        window = pl.ds(pl.multiple_of(step * tile * breadth, tile * breadth), tile * breadth)
        high[:, window] = piece_high
        low[:, window] = piece_low


def put_weight_grad(flags, parts, tap, grad):
    half = grad.shape[0] // 2
    first = (flags[SIDE] ^ flags[PIX]) & 1
    parts[first, tap] = grad[:half]
    parts[1 - first, tap] = grad[half:]


def weight_kernel(flags, x, left, ahead, grad, *rest, begin, top, bottom, skip, offset):
    if skip:
        source, cot_mine, cot_got, keep, send, total, total_skip, pole, high, low, t_high, t_low, parts, sems = rest
    else:
        behind, after, slope, keep, send, total, grad_out, pole, high, low, t_high, t_low, parts, sems = rest
        grad_first_kernel(flags, grad, behind, after, slope, grad_out)
        grad = grad_out
    rows, breadth, depth = grad.shape[0] - 2 * offset, grad.shape[1], grad.shape[2]
    put_padded(flags, x, left, ahead, pole, high, low, begin, rows + 2, top, bottom)

    def read_grad(first, count):
        return grad[pl.ds(first + offset, count)].reshape(count * breadth, depth)

    put_transposed(read_grad, rows, breadth, t_high, t_low, total, 4)
    @pl.loop(0, 3)
    def _(row_tap):
        window = pl.ds(pl.multiple_of(row_tap * breadth, breadth), rows * breadth)
        for tap in range(3):
            lanes = slice(tap * depth, (tap + 1) * depth)
            part = dot_split(t_high[...], t_low[...], high[window, lanes], low[window, lanes])
            put_weight_grad(flags, parts, row_tap * 3 + tap, part.T)

    if skip:
        def read_cot(first, count):
            window = pl.ds(first + 2, count)
            value = jnp.concatenate([cot_mine[window], cot_got[window]], axis=2)
            return value.reshape(count * breadth, depth)

        put_transposed(read_cot, rows, breadth, t_high, t_low, total_skip, 4)

        @pl.loop(0, rows)
        def _(row):
            row_high, row_low = split(source[row + 4])
            high[pl.ds(row * breadth, breadth), :depth] = row_high
            low[pl.ds(row * breadth, breadth), :depth] = row_low

        window, lanes = slice(0, rows * breadth), slice(0, depth)
        part = dot_split(t_high[...], t_low[...], high[window, lanes], low[window, lanes])
        put_weight_grad(flags, parts, 9, part.T)

    copies = [
        pltpu.make_async_copy(parts.at[k], (keep, send)[k], sems.at[k]) for k in range(2)
    ]
    for copy in copies:
        copy.start()
    for copy in copies:
        copy.wait()


def weights_kernel(flags, mine, *rest, steps, skip):
    shares, rest = rest[: steps + 1], rest[steps + 1 :]
    if skip:
        mine_skip, f_high, f_low, b_high, b_low, s_high, s_low, sb_high, sb_low, other = rest
    else:
        f_high, f_low, b_high, b_low, other = rest
    own = mine.shape[1]
    depth = 2 * own
    taps = mine.shape[0]
    count = 1 << steps
    share, share_skip = taps // count, depth // count
    unit = shares[0].shape[0]
    begin = share if skip else 0
    for piece in range(count):
        away = sum(1 << (steps - 1 - step) for step in range(steps) if piece >> step & 1)
        index = (flags[PIX] & (count - 1)) ^ away
        level = piece.bit_length()
        source = shares[level]
        at = (piece - (1 << (level - 1)) if level else 0) * unit + begin
        other[pl.ds(pl.multiple_of(index * share, 8), share)] = source[at : at + share]
        if skip:
            start = pl.multiple_of(taps + index * share_skip, 8)
            other[pl.ds(start, share_skip)] = source[at + share : at + share + share_skip]
    def both(first, second):
        return jnp.concatenate([first, second], axis=1)

    @pl.loop(0, 9)
    def _(tap):
        row_tap, column_tap = tap // 3, tap % 3
        back_row, back_column = 2 - row_tap, 2 - column_tap
        for part in range(2):
            at = pl.multiple_of(tap * depth + jnp.where(flags[SIDE] == part, 0, own), own)
            value = both(mine[pl.ds(at, own)], other[pl.ds(at, own)])
            value_high, value_low = split(value)
            place = pl.ds(pl.multiple_of(column_tap * depth + part * own, own), own)
            f_high[row_tap, place] = value_high
            f_low[row_tap, place] = value_low
            turned_high, turned_low = split(value.T)
            place = pl.ds(pl.multiple_of(back_column * depth, depth), depth)
            lanes = slice(part * own, (part + 1) * own)
            b_high[back_row, place, lanes] = turned_high
            b_low[back_row, place, lanes] = turned_low

    if skip:
        for part in range(2):
            at = pl.multiple_of(jnp.where(flags[SIDE] == part, 0, own), own)
            value = both(mine_skip[pl.ds(at, own)], other[pl.ds(pl.multiple_of(taps + at, own), own)])
            lanes = slice(part * own, (part + 1) * own)
            s_high[lanes], s_low[lanes] = split(value)
            sb_high[:, lanes], sb_low[:, lanes] = split(value.T)


def pre_kernel(flags, features, mask, marked, theirs, stats, inner, to_prev, to_next):
    rows, breadth, own = features.shape
    length = theirs.shape[0]
    start = (1 - flags[HALF]) * (rows - length)
    turned = mask[...].astype(F32)
    turned = jnp.concatenate([turned, jnp.zeros((breadth, 128 - rows), F32)], axis=1)
    none = jnp.zeros((8, own), F32)

    def fold(v):
        return jnp.sum(v.reshape(breadth // 8, 8, own), axis=0)

    def first(step, carry):
        count, total = carry
        base = step * 8
        sea_of = pltpu.roll(turned, 128 - base, 1)
        for k in range(8):
            row = base + k
            sea = jnp.broadcast_to(sea_of[:, k : k + 1], (breadth, own))
            value = features[row]
            land = jnp.where(sea > 0.5, value, NOT_SEA)
            marked[row] = land
            to_prev[pl.ds(row, 1)] = land[0:1]
            to_next[pl.ds(row, 1)] = land[breadth - 1 : breadth]
            count, total = count + fold(sea), total + fold(value * sea)
        return count, total

    count, total = lax.fori_loop(0, rows // 8, first, (none, none))
    count = jnp.sum(count, axis=0, keepdims=True)
    mean = jnp.sum(total, axis=0, keepdims=True) / jnp.maximum(count, 1.0)

    def second(step, squares):
        for k in range(8):
            value = marked[step * 8 + k]
            value = jnp.where(value > 0.1 * NOT_SEA, 0.0, value - mean)
            squares = squares + fold(value * value)
        return squares

    squares = lax.fori_loop(0, rows // 8, second, none)

    @pl.loop(0, length // 4)
    def _(step):
        theirs[pl.ds(step * 4, 4)] = marked[pl.ds(start + step * 4, 4)]

    stats[...] = jnp.zeros_like(stats)
    stats[0:1] = count
    stats[1:2] = mean
    stats[2:3] = jnp.sum(squares, axis=0, keepdims=True)
    strip = flags[SIDE] ^ flags[HALF]
    to_prev[rows:] = marked[strip * (rows - 1)]
    inner[...] = marked[pl.ds((1 - strip) * (rows - inner.shape[0]), inner.shape[0])]


def rims_kernel(flags, behind, ahead, core, stats, mine, theirs, wide):
    rows, own = behind.shape
    breadth = ahead.shape[0] - rows
    extra = (core.shape[0]) // (breadth + 2)
    length = rows // 2 + 2 * extra
    inner = extra * breadth
    at = inner
    for target in (mine, theirs):
        target[:inner] = core[:inner]
    for source, start in ((behind, inner + extra), (ahead, inner)):
        wide[:extra] = core[start : start + extra]
        wide[extra : extra + rows] = source[:rows]
        wide[extra + rows :] = core[start : start + extra]
        for target, half in ((mine, flags[HALF]), (theirs, 1 - flags[HALF])):
            target[at : at + length] = wide[pl.ds(pl.multiple_of(half * (rows // 2), 8), length)]
        at = at + length
    count, mean, squares = stats[0:1], stats[1:2], stats[2:3]
    inverse = lax.rsqrt(squares / count + EPSILON)
    for target in (mine, theirs):
        target[at : at + breadth] = ahead[rows:]
        target[at + breadth :] = jnp.zeros((8, own), F32)
        target[at + breadth : at + breadth + 1] = mean
        target[at + breadth + 1 : at + breadth + 2] = inverse


def final_kernel(flags, marked, lower, rims, stats, sums, *rest, other, parts):
    out, source, result, in_sems, out_sems = rest[-5:]
    rows, breadth, own = marked.shape
    size = rows // 2
    step = size // parts
    last = size + 2 + breadth
    count, mean = stats[0:1], stats[1:2]
    inverse = lax.rsqrt(stats[2:3] / count + EPSILON)
    first_mean, second_mean = sums[3:4] / count, sums[4:5] / count
    column = lax.broadcasted_iota(jnp.int32, (breadth, 1), 0)
    strip = flags[SIDE] ^ flags[HALF]
    edge = strip * (size - 1)
    half = 1 - flags[HALF] if other else flags[HALF]
    at_pole = flags[SIDE] == (1 if other else 0)

    def fetch(part):
        rows = pl.ds(half * size + part * step, step)
        return pltpu.make_async_copy(marked.at[rows], source.at[pl.ds(part * step, step)], in_sems.at[part])

    def store(part):
        rows = pl.ds(half * size + part * step, step)
        return pltpu.make_async_copy(result.at[pl.ds(part * step, step)], out.at[rows], out_sems.at[part])

    for part in range(parts):
        fetch(part).start()
    for part in range(parts):
        fetch(part).wait()

        @pl.loop(part * step, (part + 1) * step)
        def _(row):
            value = lower[row] + jnp.where(column == 0, rims[pl.ds(row + 1, 1)], 0.0)
            value = value + jnp.where(column == breadth - 1, rims[pl.ds(row + last + 1, 1)], 0.0)
            at_edge = jnp.where((row == edge) & at_pole, 1.0, 0.0)
            value = value + rims[size + 2 : last] * at_edge
            normed = (source[row] - mean) * inverse
            value = inverse * (value - first_mean - normed * second_mean)
            result[row] = jnp.where(source[row] > 0.1 * NOT_SEA, 0.0, value)

        store(part).start()
    for part in range(parts):
        store(part).wait()


def final_call(other, flags, marked, lower, rims, stats, sums, before=None):
    anywhere, whole = pl.BlockSpec(memory_space=pl.ANY), pl.BlockSpec(memory_space=pltpu.VMEM)
    parts = 4
    operands = [flags, marked, lower, rims, stats, sums] + ([before] if other else [])
    half = pltpu.VMEM(lower.shape, F32)
    return pl.pallas_call(
        functools.partial(final_kernel, other=other, parts=parts),
        out_shape=jax.ShapeDtypeStruct(marked.shape, F32),
        in_specs=[pl.BlockSpec(memory_space=pltpu.SMEM), anywhere] + [whole] * 4 + [anywhere] * other,
        out_specs=anywhere,
        scratch_shapes=[half, half, pltpu.SemaphoreType.DMA((parts,)), pltpu.SemaphoreType.DMA((parts,))],
        input_output_aliases={6: 0} if other else {},
        compiler_params=pltpu.CompilerParams(vmem_limit_bytes=VMEM_LIMIT),
        cost_estimate=pl.CostEstimate(flops=0, bytes_accessed=0, transcendentals=0),
        name="final_got" if other else "final_own",
    )(*operands)


def join_kernel(flags, mine, theirs, out, sems):
    size = mine.shape[0]
    one = pltpu.make_async_copy(mine, out.at[pl.ds(flags[HALF] * size, size)], sems.at[0])
    two = pltpu.make_async_copy(theirs, out.at[pl.ds((1 - flags[HALF]) * size, size)], sems.at[1])
    one.start()
    two.start()
    one.wait()
    two.wait()


def call_copy(kernel, shape, flags, *operands):
    anywhere = pl.BlockSpec(memory_space=pl.ANY)
    return pl.pallas_call(
        kernel,
        out_shape=[jax.ShapeDtypeStruct(shape, F32)],
        in_specs=[pl.BlockSpec(memory_space=pltpu.SMEM)]
        + [pl.BlockSpec(memory_space=pltpu.VMEM)] * len(operands),
        out_specs=[anywhere],
        scratch_shapes=[pltpu.SemaphoreType.DMA((len(operands),))],
        compiler_params=pltpu.CompilerParams(vmem_limit_bytes=VMEM_LIMIT),
        cost_estimate=pl.CostEstimate(flops=0, bytes_accessed=0, transcendentals=0),
        name="join",
    )(flags, *operands)


def call(kernel, shapes, scratch, flags, *operands, name=None, copied=0):
    whole = pl.BlockSpec(memory_space=pltpu.VMEM)
    shapes = [s if isinstance(s, jax.ShapeDtypeStruct) else jax.ShapeDtypeStruct(s, F32) for s in shapes]
    return pl.pallas_call(
        kernel,
        out_shape=shapes,
        in_specs=[pl.BlockSpec(memory_space=pltpu.SMEM)] + [whole] * len(operands),
        out_specs=[pl.BlockSpec(memory_space=pl.ANY)] * copied + [whole] * (len(shapes) - copied),
        scratch_shapes=scratch,
        compiler_params=pltpu.CompilerParams(vmem_limit_bytes=VMEM_LIMIT),
        cost_estimate=pl.CostEstimate(flops=0, bytes_accessed=0, transcendentals=0),
        name=name,
    )(flags, *operands)


class Place:
    def __init__(self, mesh, rows, breadth):
        self.count = mesh.shape["pix"]
        self.strips = 3 * breadth // rows
        assert mesh.shape["ch"] == 2 and self.strips == 2
        self.pix = lax.axis_index("pix")
        self.side = lax.axis_index("ch")
        self.ribbon = self.pix // self.strips % 4
        self.strip = self.pix % self.strips
        self.half = self.side ^ self.strip
        self.at_top = (self.side == 0) & (self.strip == 0)
        self.at_bottom = (self.side == 0) & (self.strip == 1)

    def ribbon_pairs(self, offset):
        pairs = []
        for index in range(self.count):
            sample, strip = index // (4 * self.strips), index % self.strips
            ribbon = (index // self.strips + offset) % 4
            pairs.append((index, (sample * 4 + ribbon) * self.strips + strip))
        return pairs

    def to_next(self, value):
        return lax.ppermute(value, "pix", self.ribbon_pairs(1))

    def to_prev(self, value):
        return lax.ppermute(value, "pix", self.ribbon_pairs(-1))

    def across(self, value):
        return lax.ppermute(value, "ch", [(0, 1), (1, 0)])

    def flip(self, value, bit):
        return lax.ppermute(value, "pix", [(i, i ^ bit) for i in range(self.count)])

    def bits(self):
        return [1 << step for step in range(self.count.bit_length() - 1)]

    def ordered(self, mine, theirs, bit):
        upper = (self.pix & bit) != 0
        return jnp.where(upper, theirs, mine), jnp.where(upper, mine, theirs)

    def near(self):
        return self.bits()[:3]

    def gathered(self, value):
        pieces = [value]
        for bit in reversed(self.near()):
            sent = pieces[0] if len(pieces) == 1 else jnp.concatenate(pieces, axis=0)
            pieces.append(self.flip(sent, bit))
        return pieces

    def members(self, bits):
        out = []
        for other in range(1, 1 << len(bits)):
            mask = sum(bit for step, bit in enumerate(bits) if other >> step & 1)
            out.append((other, [(i, i ^ mask) for i in range(self.count)]))
        return out

    def number(self, bits):
        total = 0
        for step, bit in enumerate(bits):
            total = total + (((self.pix & bit) != 0).astype(jnp.int32) << step)
        return total

    def shared(self, value, bits):
        me, length = self.number(bits), value.shape[0] >> len(bits)
        total = lax.dynamic_slice_in_dim(value, me * length, length, 0)
        parts = []
        for other, pairs in self.members(bits):
            piece = lax.dynamic_slice_in_dim(value, (me ^ other) * length, length, 0)
            parts.append(lax.ppermute(piece, "pix", pairs))
        for part in parts:
            total = total + part
        return total

    def spread(self, value, bits):
        parts = [value] + [lax.ppermute(value, "pix", pairs) for _, pairs in self.members(bits)]
        for step, bit in enumerate(bits):
            upper = (self.pix & bit) != 0
            parts = [
                jnp.where(upper, parts[k ^ (1 << step)], parts[k]) for k in range(len(parts))
            ]
        return jnp.concatenate(parts, axis=0)

    def groups(self):
        bits = self.bits()
        rest = [bits[k : k + 2] for k in range(2, len(bits), 2)]
        return [bits[:1], bits[1:2]] + rest

    def summed(self, value):
        for bit in self.bits():
            first, second = self.ordered(value, self.flip(value, bit), bit)
            value = first + second
        return value

    def part(self, value, half, start, length):
        return lax.dynamic_slice_in_dim(value, half * start, length, 0)

    def join_rows(self, mine, theirs):
        return jnp.where(
            self.half == 0,
            jnp.concatenate([mine, theirs], axis=0),
            jnp.concatenate([theirs, mine], axis=0),
        )

    def inner_rows(self, value, extra):
        edge = jnp.where(self.strip == 0, value[-extra:], value[:extra])
        return self.flip(edge, 1)


def merged_stats(place, state):
    for bit in place.bits():
        first, second = place.ordered(state, place.flip(state, bit), bit)
        total = first[0] + second[0]
        safe = jnp.maximum(total, 1.0)
        step = second[1] - first[1]
        state = jnp.stack(
            [
                total,
                (first[0] * first[1] + second[0] * second[1]) / safe,
                first[2] + second[2] + step * step * (first[0] * second[0] / safe),
            ]
            + [total] * 5
        )
    return state


def local(
    mesh, features, sea_mask, edge_flip, w_first, b_first, w_second, b_second, w_skip, b_skip,
    run_mean, run_var, cotangent,
):
    rows, breadth, own = features.shape
    place = Place(mesh, rows, breadth)
    size, depth = rows // 2, 2 * own
    taps = 9 * depth
    flip_row = jnp.sum(jnp.where((jnp.arange(4) == place.ribbon)[:, None], edge_flip, 0), axis=0)
    flipped = jnp.where(place.strip == 0, flip_row[0], flip_row[1]) == 1
    flags = jnp.stack(
        [
            jnp.where(flag, 1, 0).astype(jnp.int32)
            for flag in (place.at_top, place.at_bottom, place.side == 1, place.half == 1, flipped)
        ]
        + [place.pix.astype(jnp.int32)]
    )

    w_first, w_second = w_first.reshape(taps, own), w_second.reshape(taps, own)
    near = len(place.near())
    share, share_skip, number = taps >> near, depth >> near, place.number(place.near())
    biases = jnp.stack([b_first, b_second, b_skip])
    message = jnp.concatenate(
        [
            lax.dynamic_slice_in_dim(w_first, number * share, share, 0),
            lax.dynamic_slice_in_dim(w_second, number * share, share, 0),
            lax.dynamic_slice_in_dim(w_skip, number * share_skip, share_skip, 0),
            jnp.pad(biases, ((0, 5), (0, 0))),
        ]
    )
    message = place.across(message)
    features, message = lax.optimization_barrier((features, message))
    marked, theirs, stats, inner, to_prev, to_next = call(
        pre_kernel,
        [
            (rows, breadth, own), (size + 4, breadth, own), (8, own), (4, breadth, own),
            (rows + breadth, own), (rows, own),
        ],
        [], flags, features, sea_mask.T, name="pre",
    )
    got = place.across(theirs)
    biases = jnp.concatenate([biases, message[2 * share + share_skip :][:3]], axis=1)
    def neighbours(stats, inner, to_prev, to_next, message):
        shares = place.gathered(message[: 2 * share + share_skip])
        stats = merged_stats(place, stats)
        ahead, behind = place.to_prev(to_prev), place.to_next(to_next)

        def inner_part(value):
            return jnp.where(place.strip == 0, value[rows - 4 : rows], value[:4])

        core = jnp.concatenate(
            [inner.reshape(-1, own), inner_part(ahead), inner_part(behind)], axis=0
        )
        core = place.flip(core, 1)
        halo_mine, halo_theirs = call(
            rims_kernel, [(rim_rows, own)] * 2, [pltpu.VMEM((rows + 8, own), F32)],
            flags, behind, ahead, core, stats, name="rims",
        )
        return stats, halo_mine, halo_theirs, shares

    def block(steps, *operands):
        shapes = jax.eval_shape(steps, *operands)

        def nothing(*operands):
            return jax.tree.map(lambda leaf: jnp.zeros(leaf.shape, leaf.dtype), shapes)

        return lax.cond(edge_flip[0, 0] < 2, steps, nothing, *operands)

    rim_rows = 4 * breadth + 2 * (size + 8) + breadth + 8
    stats, halo_mine, halo_theirs, shares = block(neighbours, stats, inner, to_prev, to_next, message)
    kinds = [jax.ShapeDtypeStruct((3, 3 * depth, depth), BF16)] * 4
    first_weights = call(
        functools.partial(weights_kernel, steps=near, skip=False),
        kinds, [pltpu.VMEM((taps, own), F32)], flags, w_first, *shares,
        name="weights_first",
    )
    sea_count, batch_mean = stats[0], stats[1]
    batch_var = stats[2] / sea_count
    halo_theirs, got = lax.optimization_barrier((halo_theirs, got))
    halo_got = place.across(halo_theirs)

    extra = place.inner_rows(cotangent, 2)
    wide = jnp.concatenate([extra, cotangent, extra], axis=0)
    cot_mine = place.part(wide, place.half, size, size + 4)
    cot_theirs = place.part(wide, 1 - place.half, size, size + 4)
    cot_theirs, halo_got = lax.optimization_barrier((cot_theirs, halo_got))
    cot_got = place.across(cot_theirs)

    small = [jax.ShapeDtypeStruct((depth, depth), BF16)] * 4
    second_weights = call(
        functools.partial(weights_kernel, steps=near, skip=True),
        kinds + small, [pltpu.VMEM((taps + depth, own), F32)], flags,
        w_second, *shares, w_skip,
        name="weights_second",
    )

    def shift_scratch(blocks):
        return [pltpu.VMEM((blocks * breadth, 3 * depth), BF16) for _ in range(2)]

    def edges():
        return [pltpu.VMEM((breadth + 8, depth), F32) for _ in range(2)]

    def turned():
        return [pltpu.VMEM((depth, size * breadth), BF16) for _ in range(2)]

    def halves(count):
        return [pltpu.VMEM((2, count, own, depth), F32), pltpu.SemaphoreType.DMA((2,))]

    pole_row = [pltpu.VMEM((breadth, depth), F32)]

    scaled, x_left, x_ahead, hidden, slope_first, to_prev, to_next = call(
        functools.partial(first_kernel, tile=9),
        [
            (size + 8, breadth, depth), (size + 8, depth), (size + 8 + breadth, depth),
            (size + 6, breadth, depth), (size + 6, breadth, depth),
            (size + 6 + breadth, depth), (size + 6, depth),
        ],
        pole_row + shift_scratch(size + 8),
        flags, marked, got, halo_mine, halo_got, *first_weights[:2], biases,
        name="first",
    )
    h_ahead, h_left = place.to_prev(to_prev), place.to_next(to_next)
    out_own, out_send, slope_second = call(
        functools.partial(second_kernel, tile=4),
        [(size, breadth, own), (size, breadth, own), (size + 4, breadth, depth)],
        pole_row + shift_scratch(size + 6),
        flags, hidden, h_left, h_ahead, *second_weights[:2], biases, scaled, *second_weights[4:6],
        name="second",
    )
    out_got = place.across(out_send)

    rim_shapes = [(size + 2 + breadth, depth), (size + 2, depth)]
    upper, grad_second, to_next, to_prev = call(
        functools.partial(back_second_kernel, tile=8),
        [(size + 8, breadth, depth), (size, breadth, depth)] + rim_shapes,
        shift_scratch(size + 10) + edges(),
        flags, cot_mine, cot_got, slope_second, *second_weights[2:4],
        name="back_second",
    )
    groups = place.groups()

    def second_weights_grad(to_next, to_prev, grad_second):
        behind, after = place.to_next(to_next), place.to_prev(to_prev)
        grads = call(
            functools.partial(weight_kernel, begin=2, top=2, bottom=size + 3, skip=True, offset=0),
            [(10, own, depth)] * 2 + [(1, depth)] * 2,
            pole_row + shift_scratch(size + 2) + turned() + halves(10),
            flags, hidden, h_left, h_ahead, grad_second, scaled, cot_mine, cot_got,
            name="weight_second", copied=2,
        )
        return behind, after, *grads

    behind, after, keep, send, gb_second, gb_skip = block(
        second_weights_grad, to_next, to_prev, grad_second
    )
    out_got, send = lax.optimization_barrier((out_got, send))

    def first_weights_grad(keep, send, upper, behind, after):
        grads = call(
            functools.partial(weight_kernel, begin=3, top=3, bottom=size + 4, skip=False, offset=1),
            [(9, own, depth)] * 2 + [(1, depth), (size + 2, breadth, depth)],
            pole_row + shift_scratch(size + 2) + turned() + halves(9),
            flags, scaled, x_left, x_ahead, upper, behind, after, slope_first,
            name="weight_first", copied=2,
        )
        return (keep + place.flip(send, groups[0][0])).reshape(-1, depth), *grads

    gw_second, keep, send, gb_first, grad_first = block(
        first_weights_grad, keep, send, upper, behind, after
    )

    def input_grad(gw_second, keep, send, grad_first):
        grads = call(
            functools.partial(back_first_kernel, tile=8),
            [(size, breadth, own), (size, breadth, own)] + rim_shapes,
            [pltpu.VMEM((size + 8, breadth, depth), F32)] + shift_scratch(size + 10) + edges(),
            flags, grad_first, cot_mine, cot_got,
            *first_weights[2:4], *second_weights[6:8],
            name="back_first",
        )
        gw_first = (keep + place.flip(send, groups[0][0])).reshape(-1, depth)
        return place.shared(gw_second, groups[1]), gw_first, *grads

    gw_second, gw_first, lower_own, lower_send, to_next, to_prev = block(
        input_grad, gw_second, keep, send, grad_first
    )
    lower_got = place.across(lower_send)

    def last_sums(gw_second, gw_first, to_next, to_prev, lower_own, lower_send, out_own, out_got):
        behind, after = place.to_next(to_next), place.to_prev(to_prev)
        behind, after, gw_first, gw_second = lax.optimization_barrier((behind, after, gw_first, gw_second))
        adds = jnp.concatenate([behind, after], axis=0)
        adds_got = place.across(adds[:, own:])
        column = jnp.arange(breadth)[None, :, None]
        row = jnp.arange(size)[:, None, None]
        edge = jnp.where(place.strip == 0, 0, size - 1)
        at_pole = place.side == 0

        def with_rims(value, adds):
            last = size + 2 + breadth
            value = value + jnp.where(column == 0, adds[1 : size + 1, None], 0.0)
            value = value + jnp.where(column == breadth - 1, adds[last + 1 : last + 1 + size, None], 0.0)
            return value + jnp.where((row == edge) & at_pole, adds[None, size + 2 : last], 0.0)

        sea_weight = sea_mask.astype(F32)[:, :, None]
        own_weight = lax.dynamic_slice_in_dim(sea_weight, place.half * size, size, 0)
        source = scaled[4 : size + 4]
        parts = []
        for value, lanes in ((lower_own, slice(0, own)), (lower_send, slice(own, depth))):
            value = with_rims(value, adds[:, lanes])
            parts.append(
                jnp.stack(
                    [
                        jnp.sum(own_weight * value, axis=(0, 1)),
                        jnp.sum(source[:, :, lanes] * value, axis=(0, 1)),
                    ]
                )
            )
        zeros = jnp.zeros((3, depth), F32)
        sums = [gb_first, gb_second, gb_skip, jnp.concatenate(parts, axis=1), zeros]
        sums = place.summed(jnp.concatenate(sums, axis=0))
        sums = sums[:, :own] + place.across(sums[:, own:])

        def all_summed(grad, begin):
            for bits in groups[begin:]:
                grad = place.shared(grad, bits)
            grad = grad[:, :own] + place.across(grad[:, own:])
            for bits in reversed(groups[1:]):
                grad = place.spread(grad, bits)
            grad = grad.reshape(-1, own, own)
            other = place.flip(grad, groups[0][0])
            return jnp.concatenate(place.ordered(grad, other, groups[0][0]), axis=1)

        gw_second, gw_first = all_summed(gw_second, 2), all_summed(gw_first, 1)
        output, = call_copy(join_kernel, (rows, breadth, own), flags, out_own, out_got)
        adds_own = adds[:, :own]
        grad_half = final_call(0, flags, marked, lower_own, adds_own, stats, sums)
        return gw_second[:9], gw_second[9], gw_first, sums, adds_got, output, grad_half

    gw_second, gw_skip, gw_first, sums, adds_got, output, grad_half = last_sums(
        gw_second, gw_first, to_next, to_prev, lower_own, lower_send, out_own, out_got
    )
    late = (sums, gw_first, gw_second, gw_skip, grad_half, lower_got, adds_got)
    sums, gw_first, gw_second, gw_skip, grad_half, lower_got, adds_got = lax.optimization_barrier(late)
    grad_features = final_call(1, flags, marked, lower_got, adds_got, stats, sums, grad_half)
    new_mean = (1.0 - MOMENTUM) * run_mean + MOMENTUM * batch_mean
    new_var = (1.0 - MOMENTUM) * run_var + MOMENTUM * batch_var * sea_count / (sea_count - 1.0)
    return (
        output,
        grad_features,
        gw_first.reshape(3, 3, depth, own),
        sums[0],
        gw_second.reshape(3, 3, depth, own),
        sums[1],
        gw_skip,
        sums[2],
        new_mean,
        new_var,
    )


def solution(mesh):
    field, kernel, vector = P("pix", None, "ch"), P(None, None, None, "ch"), P("ch")
    placed = (
        field, P("pix", None), P(), kernel, vector, kernel, vector, P(None, "ch"), vector,
        vector, vector, field,
    )
    return jax.shard_map(
        functools.partial(local, mesh),
        mesh=mesh,
        in_specs=placed,
        out_specs=(
            field, field, kernel, vector, kernel, vector, P(None, "ch"), vector, vector, vector,
        ),
        check_vma=False,
    )
```

time: 499 us -> 361 us (0.72)
  local copies, waits for them, and re-layouts: 83.3 us -> 19.4 us
  waiting for transfers between devices: 135 us -> 78.7 us
  other arithmetic: 72.1 us -> 29.1 us
  Pallas kernels: 138 us -> 175 us
  starting transfers between devices: 63 us -> 54.3 us
    ppermute x9 -> x10, waiting for transfers between devices: 60.7 us -> 14.5 us  [across(): return lax.ppermute(value, 'ch', [(0, 1), (1, 0)])]
    ppermute x30 -> x17, waiting for transfers between devices: 70.1 us -> 29.1 us  [flip(): return lax.ppermute(value, 'pix', [(i, i ^ bit) for i in range(self.count)])]
    pallas_call x6 -> x13, Pallas kernels: 138 us -> 175 us  [the longest x10 163 us: call(): pl.pallas_call(kernel, out_shape=shapes, in_specs=[pl.BlockSpec(memory_sp...]
    ppermute x0 -> x16, waiting for transfers between devices: none -> 28.7 us  [the longest x8 15.9 us: shared(): parts.append(lax.ppermute(piece, 'pix', pairs))]
    ppermute x30 -> x17, starting transfers between devices: 31.6 us -> 11.1 us  [flip(): return lax.ppermute(value, 'pix', [(i, i ^ bit) for i in range(self.count)])]
    select_n x23 -> x7, other arithmetic: 18.6 us -> 1.04 us  [the longest x1 0.88 us: inner_rows(): edge = jnp.where(self.strip == 0, value[-extra:], value[:extra])]
    ppermute x0 -> x16, starting transfers between devices: none -> 17.2 us  [the longest x8 9.78 us: shared(): parts.append(lax.ppermute(piece, 'pix', pairs))]
    transpose x5 -> x0, local copies, waits for them, and re-layouts: 14.4 us -> none  [the longest x4 11 us: backward_weights(): weights[::-1, ::-1].transpose(0, 1, 3, 2).reshape(3, 3 * depth, depth)]
  transfers between devices with their start and end apart: 47 -> 51, of which waited for: 25 -> 25; matrix products, arithmetic and copies ran while one was open for 19% -> 10% of each run, Pallas kernels for 9% -> 45%
where the time goes in v2:
time: 361 us; the launch traced here: 360 us
  Pallas kernels  175 us (48%)
  waiting for transfers between devices  78.7 us (22%)
  starting transfers between devices  54.3 us (15%)
  other arithmetic  29.1 us (8%)
  local copies, waits for them, and re-layouts  19.4 us (5%)
    pallas_call x10, Pallas kernels, call(): pl.pallas_call(kernel, out_shape=shapes, in_specs=[pl.BlockSpec(memory_sp...  163 us
    ppermute x17, waiting for transfers between devices, flip(): return lax.ppermute(value, 'pix', [(i, i ^ bit) for i in range(self.count)])  29.1 us
    ppermute x8, waiting for transfers between devices, shared(): parts.append(lax.ppermute(piece, 'pix', pairs))  15.9 us
    ppermute x10, starting transfers between devices, across(): return lax.ppermute(value, 'ch', [(0, 1), (1, 0)])  15.1 us
    ppermute x10, waiting for transfers between devices, across(): return lax.ppermute(value, 'ch', [(0, 1), (1, 0)])  14.5 us
    ppermute x8, waiting for transfers between devices, spread(): lax.ppermute(value, 'pix', pairs)  12.8 us
    ppermute x17, starting transfers between devices, flip(): return lax.ppermute(value, 'pix', [(i, i ^ bit) for i in range(self.count)])  11.1 us
    ppermute x8, starting transfers between devices, shared(): parts.append(lax.ppermute(piece, 'pix', pairs))  9.78 us
  transfers between devices with their start and end apart: 51, of which 25 were waited for; matrix products, arithmetic and copies ran while one was open for 10% of the time, Pallas kernels for 45%

profile of v2, /device:TPU:0, one launch (start us, length us, event | category | flops | bytes accessed | tf_op | source)
XLA Modules:
  0.0 359.8 jit_solution(14276117883833480593)
XLA Ops:
  8.9 4.7 %collective-permute-done.15 = f32[616,128]{1,0:T(8,128)S(1)} collective-permute-done((f32[616,128]{1,0:T(8,128)S(1)}, f32[616,128]{1,0:T(8,128)S(1)}, u32[]{:S(2)}, u32[]{:S(2)}) %collective-permute-start.15) | collective-permute-done | bytes 315424 | tf_op jit(solution)/shard_map/ppermute | solution.py:638
  13.6 7.8 %pre.1 = (f32[96,64,128]{2,1,0:T(8,128)}, f32[52,64,128]{2,1,0:T(8,128)}, f32[8,128]{1,0:T(8,128)S(1)}, f32[4,64,128]{2,1,0:T(8,128)}, f32[160,128]{1,0:T(8,128)}, /*index=5*/f32[96,128]{1,0:T(8,128)}) custom-call(s32[6]{0:T(128)S(1)} %stack.84.flags, f32[96,64,128]{2,1,0:T(8,128)} %features, s32[64,96]{1,0:T(8,128)} %bitcast.63), custom_call_target="tpu_custom_call" | custom-call | tf_op jit(solution)/shard_map/pre/pallas_call | solution.py:598
  27.5 48.4 %conditional.4 = (f32[8,128]{1,0:T(8,128)}, f32[440,128]{1,0:T(8,128)S(1)}, f32[440,128]{1,0:T(8,128)}, f32[608,128]{1,0:T(8,128)}, f32[608,128]{1,0:T(8,128)}, ...) conditional(s32[]{:T(128)} %bitcast.17, () %tuple.47, (s32[]{:T(128)}, f32[8,128]{1,0:T(8,128)S(1)}, f32[96,128]{1,0:T(8,128)}, ...), branch_computations={%region_1.2_spmd, %region_2.3_spmd} | conditional | flops 862217 | bytes 16204443 | solution.py:802
  33.8 8.0 %collective-permute-done.12 = f32[608,128]{1,0:T(8,128)} collective-permute-done((f32[608,128]{1,0:T(8,128)}, f32[608,128]{1,0:T(8,128)}, u32[]{:S(2)}, u32[]{:S(2)}) %collective-permute-start.12) | collective-permute-done | bytes 311328 | tf_op jit(solution)/shard_map/cond/branch_1_fun/ppermute | solution.py:641
  48.0 11.2 %collective-permute-done.13 = f32[1216,128]{1,0:T(8,128)} collective-permute-done((f32[1216,128]{1,0:T(8,128)}, f32[1216,128]{1,0:T(8,128)}, u32[]{:S(2)}, u32[]{:S(2)}) %collective-permute-start.13) | collective-permute-done | bytes 622624 | tf_op jit(solution)/shard_map/cond/branch_1_fun/ppermute | solution.py:641
  80.1 4.2 %collective-permute-done.18.halo_got = f32[440,128]{1,0:T(8,128)} collective-permute-done((f32[440,128]{1,0:T(8,128)}, f32[440,128]{1,0:T(8,128)}, u32[]{:S(2)}, u32[]{:S(2)}) %collective-permute-start.18) | collective-permute-done | bytes 225312 | tf_op jit(solution)/shard_map/ppermute | solution.py:638
  85.3 5.5 %weights_first.1 = (bf16[3,768,256]{2,1,0:T(8,128)(2,1)}, bf16[3,768,256]{2,1,0:T(8,128)(2,1)}, bf16[3,768,256]{2,1,0:T(8,128)(2,1)}, bf16[3,768,256]{2,1,0:T(8,128)(2,1)}) custom-call(s32[6]{0:T(128)S(1)} %stack.84.flags, f32[2304,128]{1,0:T(8,128)} %bitcast.58, f32[608,128]{1,0:T(8,128)} %get-tuple-element.232.rest_0_, ...), custom_call_target="tpu_custom_call" | custom-call | tf_op jit(solution)/shard_map/weights_first/pallas_call | solution.py:598
  90.8 23.4 %first.1 = (f32[56,64,256]{2,1,0:T(8,128)S(1)}, f32[56,256]{1,0:T(8,128)}, f32[120,256]{1,0:T(8,128)}, f32[54,64,256]{2,1,0:T(8,128)}, f32[54,64,256]{2,1,0:T(8,...) custom-call(s32[6]{0:T(128)S(1)} %stack.84.flags, f32[96,64,128]{2,1,0:T(8,128)} %get-tuple-element.220.marked, ...), custom_call_target="tpu_custom_call" | custom-call | tf_op jit(solution)/shard_map/first/pallas_call | solution.py:598
  116.3 5.5 %weights_second.1 = (bf16[3,768,256]{2,1,0:T(8,128)(2,1)}, bf16[3,768,256]{2,1,0:T(8,128)(2,1)}, bf16[3,768,256]{2,1,0:T(8,128)(2,1)}, bf16[3,768,256]{2,1,0:T(8...) custom-call(s32[6]{0:T(128)S(1)} %stack.84.flags, ...), custom_call_target="tpu_custom_call" | custom-call | tf_op jit(solution)/shard_map/weights_second/pallas_call | solution.py:598
  121.9 24.1 %second.1 = (f32[48,64,128]{2,1,0:T(8,128)}, f32[48,64,128]{2,1,0:T(8,128)}, f32[52,64,256]{2,1,0:T(8,128)}) custom-call(s32[6]{0:T(128)S(1)} %stack.84.flags, f32[54,64,256]{2,1,0:T(8,128)} %get-tuple-element.238.x, f32[54,256]{1,0:T(8,128)S(1)} %collective-permute-done.19.left, f32[118,256]{1,0:T(8,128)S(1)} %collective-permute-done.20.ahead, ...), custom_call_target="tpu_custom_call" | custom-call | tf_op jit(solution)/shard_map/second/pallas_call | solution.py:598
  148.7 23.5 %back_second.1 = (f32[56,64,256]{2,1,0:T(8,128)}, f32[48,64,256]{2,1,0:T(8,128)}, f32[114,256]{1,0:T(8,128)}, f32[50,256]{1,0:T(8,128)}) custom-call(s32[6]{0:T(128)S(1)} %stack.84.flags, f32[52,64,128]{2,1,0:T(8,128)} %get-tuple-element.314.cot_mine, f32[52,64,128]{2,1,0:T(8,128)} %collective-permute-done.22.cot_got, ...), custom_call_target="tpu_custom_call" | custom-call | tf_op jit(solution)/shard_map/back_second/pallas_call | solution.py:598
  172.3 28.1 %conditional.5 = (f32[114,256]{1,0:T(8,128)}, f32[50,256]{1,0:T(8,128)}, f32[10,128,256]{2,1,0:T(8,128)}, f32[10,128,256]{2,1,0:T(8,128)}, f32[1,256]{1,0:T(1,128)S(1)}, /*index=5*/f32[1,256]{1,0:T(1,128)S(1)}) conditional(s32[]{:T(128)} %bitcast.17, () %tuple.51, (f32[114,256]{1,0:T(8,128)}, f32[50,256]{1,0:T(8,128)}, s32[6]{0:T(128)S(1)}, ...), branch_computations={%region_3.4_spmd, %region_4.5_spmd} | conditional | bytes 2791496 | solution.py:802
  175.3 24.8 %weight_second.1 = (f32[10,128,256]{2,1,0:T(8,128)}, f32[10,128,256]{2,1,0:T(8,128)}, f32[1,256]{1,0:T(1,128)S(1)}, f32[1,256]{1,0:T(1,128)S(1)}) custom-call(s32[6]{0:T(128)S(1)} %get-tuple-element.92.flags, f32[54,64,256]{2,1,0:T(8,128)} %get-tuple-element.93.x, f32[54,256]{1,0:T(8,128)S(1)} %get-tuple-element.94.left, ...), custom_call_target="tpu_custom_call" | custom-call | tf_op jit(solution)/shard_map/cond/branch_1_fun/weight_second/pallas_call | solution.py:598
  200.4 27.5 %conditional.6 = (f32[1280,256]{1,0:T(8,128)S(1)}, f32[9,128,256]{2,1,0:T(8,128)}, f32[9,128,256]{2,1,0:T(8,128)}, f32[1,256]{1,0:T(1,128)S(1)}, f32[50,64,256]{2,1,0:T(8,128)}) conditional(s32[]{:T(128)} %bitcast.17, () %tuple.54, (f32[10,128,256]{2,1,0:T(8,128)}, f32[10,128,256]{2,1,0:T(8,128)}, s32[6]{0:T(128)S(1)}, f32[56,64,256]{2,1,0:T(8,128)}, ...), branch_computations={%region_5.6_spmd, %region_6.7_spmd} | conditional | flops 327680 | bytes 14418028 | solution.py:802
  200.5 24.4 %weight_first.1 = (f32[9,128,256]{2,1,0:T(8,128)}, f32[9,128,256]{2,1,0:T(8,128)}, f32[1,256]{1,0:T(1,128)S(1)}, f32[50,64,256]{2,1,0:T(8,128)}) custom-call(s32[6]{0:T(128)S(1)} %get-tuple-element.106.flags, f32[56,64,256]{2,1,0:T(8,128)} %get-tuple-element.107.x, f32[56,256]{1,0:T(8,128)} %get-tuple-element.108.left, f32[120,256]{1,0:T(8,128)} %get-tuple-element.109.ahead, ...), custom_call_target="tpu_custom_call" | custom-call | tf_op jit(solution)/shard_map/cond/branch_1_fun/weight_first/pallas_call | solution.py:598
  227.9 30.8 %conditional.7 = (f32[640,256]{1,0:T(8,128)}, f32[1152,256]{1,0:T(8,128)}, f32[48,64,128]{2,1,0:T(8,128)S(1)}, f32[48,64,128]{2,1,0:T(8,128)}, f32[114,256]{1,0:T(8,128)}, /*index=5*/f32[50,256]{1,0:T(8,128)}) conditional(s32[]{:T(128)} %bitcast.17, () %tuple.56, (s32[]{:T(128)}, f32[1280,256]{1,0:T(8,128)S(1)}, f32[9,128,256]{2,1,0:T(8,128)}, ...), branch_computations={%region_7.8_spmd, %region_8.9_spmd} | conditional | flops 458765 | bytes 19398962 | solution.py:802
  231.1 22.6 %back_first.1 = (f32[48,64,128]{2,1,0:T(8,128)S(1)}, f32[48,64,128]{2,1,0:T(8,128)}, f32[114,256]{1,0:T(8,128)}, f32[50,256]{1,0:T(8,128)}) custom-call(s32[6]{0:T(128)S(1)} %get-tuple-element.122.flags, f32[50,64,256]{2,1,0:T(8,128)} %get-tuple-element.123.grad, f32[52,64,128]{2,1,0:T(8,128)S(1)} %get-tuple-element.124.cot_mine, ...), custom_call_target="tpu_custom_call" | custom-call | tf_op jit(solution)/shard_map/cond/branch_1_fun/back_first/pallas_call | solution.py:598
  285.8 5.0 %collective-permute-done.28 = f32[8,256]{1,0:T(8,128)S(1)} collective-permute-done((f32[8,256]{1,0:T(8,128)S(1)}, f32[8,256]{1,0:T(8,128)S(1)}, u32[]{:S(2)}, u32[]{:S(2)}) %collective-permute-start.28) | collective-permute-done | bytes 8224 | tf_op jit(solution)/shard_map/ppermute | solution.py:641
  293.2 5.7 %collective-permute-done.41 = f32[160,256]{1,0:T(8,128)S(1)} collective-permute-done((f32[160,256]{1,0:T(8,128)S(1)}, f32[160,256]{1,0:T(8,128)S(1)}, u32[]{:S(2)}, u32[]{:S(2)}) %collective-permute-start.41) | collective-permute-done | bytes 163872 | tf_op jit(solution)/shard_map/ppermute | solution.py:679
  305.2 5.7 %collective-permute-done.43 = f32[160,128]{1,0:T(8,128)S(1)} collective-permute-done((f32[160,128]{1,0:T(8,128)S(1)}, f32[160,128]{1,0:T(8,128)S(1)}, u32[]{:S(2)}, u32[]{:S(2)}) %collective-permute-start.43) | collective-permute-done | bytes 81952 | tf_op jit(solution)/shard_map/ppermute | solution.py:638
  312.8 8.2 %collective-permute-done.32 = f32[144,256]{1,0:T(8,128)S(1)} collective-permute-done((f32[144,256]{1,0:T(8,128)S(1)}, f32[144,256]{1,0:T(8,128)S(1)}, u32[]{:S(2)}, u32[]{:S(2)}) %collective-permute-start.32) | collective-permute-done | bytes 147488 | tf_op jit(solution)/shard_map/ppermute | solution.py:679
  337.4 5.1 %collective-permute-done.47 = f32[640,128]{1,0:T(8,128)S(1)} collective-permute-done((f32[640,128]{1,0:T(8,128)S(1)}, f32[640,128]{1,0:T(8,128)S(1)}, u32[]{:S(2)}, u32[]{:S(2)}) %collective-permute-start.47) | collective-permute-done | bytes 327712 | tf_op jit(solution)/shard_map/ppermute | solution.py:685
  346.5 3.6 final_own.1.rest_0_
  355.5 4.2 %final_got.1 = f32[96,64,128]{2,1,0:T(8,128)} custom-call(s32[6]{0:T(128)S(1)} %stack.84.flags, f32[96,64,128]{2,1,0:T(8,128)} %get-tuple-element.220.marked, f32[48,64,128]{2,1,0:T(8,128)} %collective-permute-done.49.lower, f32[164,128]{1,0:T(8,128)} %copy-done.10, f32[8,128]{1,0:T(8,128)} %get-tuple-element.286.stats, ...), custom_call_target="tpu_custom_call", output_to_operand_aliasing={{}: (6, {})} | custom-call | tf_op jit(solution)/shard_map/final_got/pallas_call | solution.py:557
  (216 shorter events, 129.1 us)
Async XLA Ops:
  3.1 10.5 %collective-permute-start.15 = (f32[616,128]{1,0:T(8,128)S(1)}, f32[616,128]{1,0:T(8,128)S(1)}, u32[]{:S(2)}, u32[]{:S(2)}) collective-permute-start(f32[616,128]{1,0:T(8,128)S(1)} %pad_maximum_fusion.7), channel_id=1, source_target_pairs={{0,1},{1,0},{2,3},{3,2},{4,5},{5,4},{6,7},{7,6},{8,9},{9,8},{10,11... | collective-permute-start | bytes 946184 | tf_op jit(solution)/shard_map/ppermute | solution.py:638
  21.4 54.5 %collective-permute-start.16 = (f32[52,64,128]{2,1,0:T(8,128)}, f32[52,64,128]{2,1,0:T(8,128)}, u32[]{:S(2)}, u32[]{:S(2)}) collective-permute-start(f32[52,64,128]{2,1,0:T(8,128)} %get-tuple-element.227), channel_id=1, source_target_pairs={{0,1},{1,0},{2,3},{3,2},{4,5},{5,4},{6,7},{7,6},{8,9},{9,8},{10,11... | collective-permute-start | bytes 5111816 | tf_op jit(solution)/shard_map/ppermute | solution.py:638
  32.2 9.6 %collective-permute-start.12 = (f32[608,128]{1,0:T(8,128)}, f32[608,128]{1,0:T(8,128)}, u32[]{:S(2)}, u32[]{:S(2)}) collective-permute-start(f32[608,128]{1,0:T(8,128)} %slice.192), channel_id=1, source_target_pairs={{0,8},{2,10},{4,12},{6,14},{8,0},{10,2},{12,4},{14,6},{16,24},{18,... | collective-permute-start | bytes 933896 | tf_op jit(solution)/shard_map/cond/branch_1_fun/ppermute | solution.py:641
  43.8 15.5 %collective-permute-start.13 = (f32[1216,128]{1,0:T(8,128)}, f32[1216,128]{1,0:T(8,128)}, u32[]{:S(2)}, u32[]{:S(2)}) collective-permute-start(f32[1216,128]{1,0:T(8,128)} %pad_maximum_fusion.1), channel_id=1, source_target_pairs={{0,4},{2,6},{4,0},{6,2},{8,12},{10,14},{12,8},{14,10},{16,20},{18,... | collective-permute-start | bytes 1867784 | tf_op jit(solution)/shard_map/cond/branch_1_fun/ppermute | solution.py:641
  61.6 14.3 %collective-permute-start.14 = (f32[2432,128]{1,0:T(8,128)}, f32[2432,128]{1,0:T(8,128)}, u32[]{:S(2)}, u32[]{:S(2)}) collective-permute-start(f32[2432,128]{1,0:T(8,128)} %pad_maximum_fusion), channel_id=1, source_target_pairs={{0,2},{2,0},{4,6},{6,4},{8,10},{10,8},{12,14},{14,12},{16,18},{18,... | collective-permute-start | bytes 3735560 | tf_op jit(solution)/shard_map/cond/branch_1_fun/ppermute | solution.py:641
  84.2 64.5 %collective-permute-start.22 = (f32[52,64,128]{2,1,0:T(8,128)}, f32[52,64,128]{2,1,0:T(8,128)}, u32[]{:S(2)}, u32[]{:S(2)}) collective-permute-start(f32[52,64,128]{2,1,0:T(8,128)} %get-tuple-element.248), channel_id=1, source_target_pairs={{0,1},{1,0},{2,3},{3,2},{4,5},{5,4},{6,7},{7,6},{8,9},{9,8},{10,11... | collective-permute-start | bytes 5111816 | tf_op jit(solution)/shard_map/ppermute | solution.py:638
  145.9 54.4 %collective-permute-start.21 = (f32[48,64,128]{2,1,0:T(8,128)}, f32[48,64,128]{2,1,0:T(8,128)}, u32[]{:S(2)}, u32[]{:S(2)}) collective-permute-start(f32[48,64,128]{2,1,0:T(8,128)} %get-tuple-element.247), channel_id=1, source_target_pairs={{0,1},{1,0},{2,3},{3,2},{4,5},{5,4},{6,7},{7,6},{8,9},{9,8},{10,11... | collective-permute-start | bytes 4718600 | tf_op jit(solution)/shard_map/ppermute | solution.py:638
  172.3 27.8 %collective-permute-start = (f32[114,256]{1,0:T(8,128)}, f32[114,256]{1,0:T(8,128)}, u32[]{:S(2)}, u32[]{:S(2)}) collective-permute-start(f32[114,256]{1,0:T(8,128)} %get-tuple-element.90), channel_id=1, source_target_pairs={{0,4},{2,6},{4,8},{6,10},{8,12},{10,14},{12,0},{14,2},{16,20},{18,... | collective-permute-start | bytes 350216 | tf_op jit(solution)/shard_map/cond/branch_1_fun/ppermute | solution.py:632
  175.1 25.0 %collective-permute-start.1 = (f32[50,256]{1,0:T(8,128)}, f32[50,256]{1,0:T(8,128)}, u32[]{:S(2)}, u32[]{:S(2)}) collective-permute-start(f32[50,256]{1,0:T(8,128)} %get-tuple-element.91), channel_id=1, source_target_pairs={{0,12},{2,14},{4,0},{6,2},{8,4},{10,6},{12,8},{14,10},{16,28},{18,... | collective-permute-start | bytes 153608 | tf_op jit(solution)/shard_map/cond/branch_1_fun/ppermute | solution.py:635
  200.4 24.5 %collective-permute-start.2 = (f32[10,128,256]{2,1,0:T(8,128)}, f32[10,128,256]{2,1,0:T(8,128)S(1)}, u32[]{:S(2)}, u32[]{:S(2)}) collective-permute-start(f32[10,128,256]{2,1,0:T(8,128)} %get-tuple-element.105), channel_id=1, source_target_pairs={{0,2},{2,0},{4,6},{6,4},{8,10},{10,8},{12,14},{14,12},{16,18},{18,... | collective-permute-start | bytes 3932168 | tf_op jit(solution)/shard_map/cond/branch_1_fun/ppermute | solution.py:641
  228.0 28.0 %collective-permute-start.4 = (f32[9,128,256]{2,1,0:T(8,128)}, f32[9,128,256]{2,1,0:T(8,128)}, u32[]{:S(2)}, u32[]{:S(2)}) collective-permute-start(f32[9,128,256]{2,1,0:T(8,128)} %get-tuple-element.121), channel_id=1, source_target_pairs={{0,2},{2,0},{4,6},{6,4},{8,10},{10,8},{12,14},{14,12},{16,18},{18,... | collective-permute-start | bytes 3538952 | tf_op jit(solution)/shard_map/cond/branch_1_fun/ppermute | solution.py:641
  229.3 24.4 %collective-permute-start.3 = (f32[640,256]{1,0:T(8,128)}, f32[640,256]{1,0:T(8,128)}, u32[]{:S(2)}, u32[]{:S(2)}) collective-permute-start(f32[640,256]{1,0:T(8,128)} %constant_dynamic-slice_fusion), channel_id=1, source_target_pairs={{0,4},{2,6},{4,0},{6,2},{8,12},{10,14},{12,8},{14,10},{16,20},{18,... | collective-permute-start | bytes 1966088 | tf_op jit(solution)/shard_map/cond/branch_1_fun/ppermute | solution.py:679
  270.3 83.9 %collective-permute-start.49 = (f32[48,64,128]{2,1,0:T(8,128)}, f32[48,64,128]{2,1,0:T(8,128)}, u32[]{:S(2)}, u32[]{:S(2)}) collective-permute-start(f32[48,64,128]{2,1,0:T(8,128)} %get-tuple-element.283), channel_id=1, source_target_pairs={{0,1},{1,0},{2,3},{3,2},{4,5},{5,4},{6,7},{7,6},{8,9},{9,8},{10,11... | collective-permute-start | bytes 4718600 | tf_op jit(solution)/shard_map/ppermute | solution.py:638
  275.8 26.3 %collective-permute-start.30 = (f32[576,256]{1,0:T(8,128)S(1)}, f32[576,256]{1,0:T(8,128)S(1)}, u32[]{:S(2)}, u32[]{:S(2)}) collective-permute-start(f32[576,256]{1,0:T(8,128)S(1)} %constant_dynamic-slice_fusion.7), channel_id=1, source_target_pairs={{0,4},{2,6},{4,0},{6,2},{8,12},{10,14},{12,8},{14,10},{16,20},{18,... | collective-permute-start | bytes 1769480 | tf_op jit(solution)/shard_map/ppermute | solution.py:679
  281.7 9.1 %collective-permute-start.28 = (f32[8,256]{1,0:T(8,128)S(1)}, f32[8,256]{1,0:T(8,128)S(1)}, u32[]{:S(2)}, u32[]{:S(2)}) collective-permute-start(f32[8,256]{1,0:T(8,128)S(1)} %select_add_fusion.3), channel_id=1, source_target_pairs={{0,16},{2,18},{4,20},{6,22},{8,24},{10,26},{12,28},{14,30},{16,0},... | collective-permute-start | bytes 24584 | tf_op jit(solution)/shard_map/ppermute | solution.py:641
  282.7 8.9 %collective-permute-start.42 = (f32[160,256]{1,0:T(8,128)S(1)}, f32[160,256]{1,0:T(8,128)S(1)}, u32[]{:S(2)}, u32[]{:S(2)}) collective-permute-start(f32[160,256]{1,0:T(8,128)S(1)} %get-tuple-element.323), channel_id=1, source_target_pairs={{0,24},{2,26},{4,28},{6,30},{8,16},{10,18},{12,20},{14,22},{16,8},... | collective-permute-start | bytes 491528 | tf_op jit(solution)/shard_map/ppermute | solution.py:679
  285.8 13.1 %collective-permute-start.41 = (f32[160,256]{1,0:T(8,128)S(1)}, f32[160,256]{1,0:T(8,128)S(1)}, u32[]{:S(2)}, u32[]{:S(2)}) collective-permute-start(f32[160,256]{1,0:T(8,128)S(1)} %get-tuple-element.324), channel_id=1, source_target_pairs={{0,16},{2,18},{4,20},{6,22},{8,24},{10,26},{12,28},{14,30},{16,0},... | collective-permute-start | bytes 491528 | tf_op jit(solution)/shard_map/ppermute | solution.py:679
  291.6 62.5 %collective-permute-start.50 = (f32[164,128]{1,0:T(8,128)S(1)}, f32[164,128]{1,0:T(8,128)S(1)}, u32[]{:S(2)}, u32[]{:S(2)}) collective-permute-start(f32[164,128]{1,0:T(8,128)S(1)} %get-tuple-element.338), channel_id=1, source_target_pairs={{0,1},{1,0},{2,3},{3,2},{4,5},{5,4},{6,7},{7,6},{8,9},{9,8},{10,11... | collective-permute-start | bytes 251912 | tf_op jit(solution)/shard_map/ppermute | solution.py:638
  300.4 10.5 %collective-permute-start.43 = (f32[160,128]{1,0:T(8,128)S(1)}, f32[160,128]{1,0:T(8,128)S(1)}, u32[]{:S(2)}, u32[]{:S(2)}) collective-permute-start(f32[160,128]{1,0:T(8,128)S(1)} %slice.262), channel_id=1, source_target_pairs={{0,1},{1,0},{2,3},{3,2},{4,5},{5,4},{6,7},{7,6},{8,9},{9,8},{10,11... | collective-permute-start | bytes 245768 | tf_op jit(solution)/shard_map/ppermute | solution.py:638
  305.2 15.8 %collective-permute-start.32 = (f32[144,256]{1,0:T(8,128)S(1)}, f32[144,256]{1,0:T(8,128)S(1)}, u32[]{:S(2)}, u32[]{:S(2)}) collective-permute-start(f32[144,256]{1,0:T(8,128)S(1)} %get-tuple-element.329), channel_id=1, source_target_pairs={{0,16},{2,18},{4,20},{6,22},{8,24},{10,26},{12,28},{14,30},{16,0},... | collective-permute-start | bytes 442376 | tf_op jit(solution)/shard_map/ppermute | solution.py:679
  310.9 10.7 %collective-permute-start.31 = (f32[144,256]{1,0:T(8,128)S(1)}, f32[144,256]{1,0:T(8,128)S(1)}, u32[]{:S(2)}, u32[]{:S(2)}) collective-permute-start(f32[144,256]{1,0:T(8,128)S(1)} %get-tuple-element.327), channel_id=1, source_target_pairs={{0,8},{2,10},{4,12},{6,14},{8,0},{10,2},{12,4},{14,6},{16,24},{18,... | collective-permute-start | bytes 442376 | tf_op jit(solution)/shard_map/ppermute | solution.py:679
  312.0 9.7 %collective-permute-start.44 = (f32[160,128]{1,0:T(8,128)S(1)}, f32[160,128]{1,0:T(8,128)S(1)}, u32[]{:S(2)}, u32[]{:S(2)}) collective-permute-start(f32[160,128]{1,0:T(8,128)S(1)} %slice_add_fusion.4), channel_id=1, source_target_pairs={{0,24},{2,26},{4,28},{6,30},{8,16},{10,18},{12,20},{14,22},{16,8},... | collective-permute-start | bytes 245768 | tf_op jit(solution)/shard_map/ppermute | solution.py:685
  333.2 12.6 %collective-permute-start.29 = (f32[8,128]{1,0:T(8,128)S(1)}, f32[8,128]{1,0:T(8,128)S(1)}, u32[]{:S(2)}, u32[]{:S(2)}) collective-permute-start(f32[8,128]{1,0:T(8,128)S(1)} %slice.258), channel_id=1, source_target_pairs={{0,1},{1,0},{2,3},{3,2},{4,5},{5,4},{6,7},{7,6},{8,9},{9,8},{10,11... | collective-permute-start | bytes 12296 | tf_op jit(solution)/shard_map/ppermute | solution.py:638
  336.6 9.1 %collective-permute-start.38 = (f32[576,128]{1,0:T(8,128)S(1)}, f32[576,128]{1,0:T(8,128)S(1)}, u32[]{:S(2)}, u32[]{:S(2)}) collective-permute-start(f32[576,128]{1,0:T(8,128)S(1)} %pad_maximum_fusion.8), channel_id=1, source_target_pairs={{0,4},{2,6},{4,0},{6,2},{8,12},{10,14},{12,8},{14,10},{16,20},{18,... | collective-permute-start | bytes 884744 | tf_op jit(solution)/shard_map/ppermute | solution.py:685
  (45 other events, 295.8 us)
